TPU v7x, 256 devices: a whole 4x4x8 slice. The times are simulated.
256 devices in a mesh: dp: 2 (over core), ctx: 32 (over z, x), head: 4 (over y).
Axes of the slice: x: 4, y: 4, z: 8, core: 2. Of those that a mesh axis runs over, the one named last changes fastest.
Arguments:
- query_rows: bfloat16 [4096, 3072], P(('dp', 'ctx', 'head')), parts along dimension 0, may hold values from -6 to 6
- key_rows: bfloat16 [16384, 512], P(('dp', 'ctx'), 'head'), parts along dimension 0, may hold values from -6 to 6
- value_rows: bfloat16 [16384, 512], P(('dp', 'ctx'), 'head'), parts along dimension 0, may hold values from -6 to 6
- output_rows: bfloat16 [4096, 3072], P(('dp', 'ctx', 'head')), parts along dimension 0, may hold values from -1.5 to 1.5
- grad_out: bfloat16 [4096, 3072], P(('dp', 'ctx', 'head')), parts along dimension 0, may hold values from -768 to 768
- log_norm: float32 [4096, 24], P(('dp', 'ctx', 'head')), parts along dimension 0
- mask_table: int32 [32, 5], P('dp'), parts along dimension 0, may hold values from 0 to 8192, as said below
- key_order: int32 [256], P('dp'), parts along dimension 0, may hold values from 0 to 127, each once
- query_order: int32 [256], P('dp'), parts along dimension 0, may hold values from 0 to 127, each once
Outputs:
- grad_query: bfloat16 [4096, 3072], P(('dp', 'ctx', 'head')), parts along dimension 0
- grad_key: bfloat16 [16384, 512], P(('dp', 'ctx'), 'head'), parts along dimension 0
- grad_value: bfloat16 [16384, 512], P(('dp', 'ctx'), 'head'), parts along dimension 0
There are 2 independent parts, one for each index of `dp`. A program takes and returns all parts, laid end to end along the dimension named above; each array names one. Nothing has to cross between parts.
Inputs may be any that keep to these rules, and one draw needn't show every extreme that they name: `mask_table`: row s covers the slab positions 6144 + s * 128 (column 0) up to 6144 + (s + 1) * 128 (column 1, exclusive); column 3 equals column 1; column 2 is at most column 0; column 4 is 0 (every key in the range allowed) or 1 (only keys at or before the query's own position); the last row has kind 0. `key_order`: each stretch number appears once. `query_order`: each stretch number appears once.
All inputs are finite; a program needn't handle non-finite values.
Results may differ from a plain program's by a relative error of at most 0.0053.
Values may be sent and summed in bfloat16 or wider, within the bound.
A program may use at most 64 MiB of HBM per device.

v0:
```python
import math

import jax
import jax.numpy as jnp
from jax import lax
from jax.sharding import PartitionSpec as P

HEAD_DIM = 128
DISPATCH = 4
KCHUNK = 64
QCHUNK = 16


def stretch_positions(stretch_order, stretch_width, offset):
    within = jnp.arange(stretch_width, dtype=jnp.int32)
    return offset + (stretch_order[:, None] * stretch_width + within[None, :]).reshape(-1)


def slice_bounds(query_pos, mask_table):
    inside = (
        (query_pos[:, None] >= mask_table[None, :, 0])
        & (query_pos[:, None] < mask_table[None, :, 1])
    ).astype(jnp.int32)
    key_low = jnp.sum(inside * mask_table[None, :, 2], axis=1)
    key_high = jnp.sum(inside * mask_table[None, :, 3], axis=1)
    causal = jnp.sum(inside * mask_table[None, :, 4], axis=1)
    return (key_low, key_high, causal)


def allowed_pairs(query_pos, key_low, key_high, causal, key_pos):
    key_grid = key_pos[None, :]
    return (
        (key_grid >= key_low[:, None])
        & (key_grid < key_high[:, None])
        & ((causal[:, None] == 0) | (key_grid <= query_pos[:, None]))
    )


def pair_terms(query_blk, grad_blk, norm_blk, delta_blk, allowed, key_loc, value_loc, score_scale):
    row_count, heads_loc, head_dim = query_blk.shape
    kv_loc = key_loc.shape[1]
    group = heads_loc // kv_loc
    query_grp = query_blk.reshape(row_count, kv_loc, group, head_dim)
    grad_grp = grad_blk.reshape(row_count, kv_loc, group, head_dim)
    norm_grp = norm_blk.reshape(row_count, kv_loc, group).transpose(1, 2, 0)
    delta_grp = delta_blk.reshape(row_count, kv_loc, group).transpose(1, 2, 0)
    scores = (
        jnp.einsum("qhgd,khd->hgqk", query_grp, key_loc, preferred_element_type=jnp.float32)
        * score_scale
    )
    weights = jnp.where(
        allowed[None, None], jnp.exp(scores - norm_grp[:, :, :, None]), jnp.float32(0.0)
    )
    dprobs = jnp.einsum("qhgd,khd->hgqk", grad_grp, value_loc, preferred_element_type=jnp.float32)
    dscore = (weights * (dprobs - delta_grp[:, :, :, None])).astype(jnp.bfloat16)
    results = []
    query_term = (
        jnp.einsum("hgqk,khd->qhgd", dscore, key_loc, preferred_element_type=jnp.float32)
        * score_scale
    )
    results.append(query_term.reshape(row_count, heads_loc, head_dim))
    results.append(
        jnp.einsum("hgqk,qhgd->khd", dscore, query_grp, preferred_element_type=jnp.float32)
        * score_scale
    )
    results.append(
        jnp.einsum(
            "hgqk,qhgd->khd",
            weights.astype(jnp.bfloat16),
            grad_grp,
            preferred_element_type=jnp.float32,
        )
    )
    return tuple(results)


def masked_terms(
    query_blk, grad_blk, norm_blk, delta_blk, allowed, key_loc, value_loc, score_scale
):
    return pair_terms(
        query_blk, grad_blk, norm_blk, delta_blk, allowed, key_loc, value_loc, score_scale
    )


def local(
    query_rows,
    key_rows,
    value_rows,
    output_rows,
    grad_out,
    log_norm,
    mask_table,
    key_order,
    query_order,
):
    score_scale = 1.0 / math.sqrt(HEAD_DIM)
    heads_all = log_norm.shape[1]
    local_rows = query_rows.shape[0]
    delta_rows = jnp.sum(
        (grad_out.astype(jnp.float32) * output_rows.astype(jnp.float32)).reshape(
            local_rows, heads_all, HEAD_DIM
        ),
        axis=2,
    )
    query_loc, grad_loc = (
        lax.all_to_all(query_rows, "head", split_axis=1, concat_axis=0, tiled=True),
        lax.all_to_all(grad_out, "head", split_axis=1, concat_axis=0, tiled=True),
    )
    norm_loc, delta_loc = (
        lax.all_to_all(log_norm, "head", split_axis=1, concat_axis=0, tiled=True),
        lax.all_to_all(delta_rows, "head", split_axis=1, concat_axis=0, tiled=True),
    )
    keys_total = key_order.shape[0] * KCHUNK
    queries_total = query_order.shape[0] * QCHUNK
    heads_loc = query_loc.shape[1] // HEAD_DIM
    kv_loc = key_rows.shape[1] // HEAD_DIM
    key_count = key_rows.shape[0]
    query_all, grad_all = (
        lax.all_gather(query_loc, "ctx", axis=0, tiled=True),
        lax.all_gather(grad_loc, "ctx", axis=0, tiled=True),
    )
    norm_all, delta_all = (
        lax.all_gather(norm_loc, "ctx", axis=0, tiled=True),
        lax.all_gather(delta_loc, "ctx", axis=0, tiled=True),
    )
    own_stretches = lax.dynamic_slice_in_dim(key_order, lax.axis_index("ctx") * DISPATCH, DISPATCH)
    key_pos = stretch_positions(own_stretches, KCHUNK, 0)
    query_pos = stretch_positions(query_order, QCHUNK, keys_total - queries_total)
    key_low, key_high, causal = slice_bounds(query_pos, mask_table)
    key_loc = key_rows.reshape(key_count, kv_loc, HEAD_DIM)
    value_loc = value_rows.reshape(key_count, kv_loc, HEAD_DIM)
    block_rows = math.gcd(queries_total, 256)
    block_count = queries_total // block_rows

    def as_blocks(values_in):
        return values_in.reshape((block_count, block_rows) + values_in.shape[1:])

    slab_blocks = (
        as_blocks(query_all.reshape(queries_total, heads_loc, HEAD_DIM)),
        as_blocks(grad_all.reshape(queries_total, heads_loc, HEAD_DIM)),
        as_blocks(norm_all),
        as_blocks(delta_all),
        as_blocks(query_pos),
        as_blocks(key_low),
        as_blocks(key_high),
        as_blocks(causal),
    )

    def slab_terms(block_items):
        query_blk, grad_blk, norm_blk, delta_blk, pos_blk, low_blk, high_blk, causal_blk = (
            block_items
        )
        allowed = allowed_pairs(pos_blk, low_blk, high_blk, causal_blk, key_pos)
        return masked_terms(
            query_blk, grad_blk, norm_blk, delta_blk, allowed, key_loc, value_loc, score_scale
        )

    zeros_keys = jnp.zeros((key_count, kv_loc, HEAD_DIM), jnp.float32)

    def joint_step(totals, block_items):
        query_part, key_part, value_part = slab_terms(block_items)
        return ((totals[0] + key_part, totals[1] + value_part), query_part)

    totals, query_parts = lax.scan(joint_step, (zeros_keys, zeros_keys), slab_blocks)
    query_sum = lax.psum_scatter(
        query_parts.reshape(queries_total, heads_loc * HEAD_DIM),
        "ctx",
        scatter_dimension=0,
        tiled=True,
    )
    grad_key = totals[0].astype(jnp.bfloat16).reshape(key_count, kv_loc * HEAD_DIM)
    grad_value = totals[1].astype(jnp.bfloat16).reshape(key_count, kv_loc * HEAD_DIM)
    grad_query = lax.all_to_all(
        query_sum.astype(jnp.bfloat16), "head", split_axis=0, concat_axis=1, tiled=True
    )
    return (grad_query, grad_key, grad_value)


def solution(mesh):
    return jax.shard_map(
        local,
        mesh=mesh,
        in_specs=(
            P(("dp", "ctx", "head"), None),
            P(("dp", "ctx"), "head"),
            P(("dp", "ctx"), "head"),
            P(("dp", "ctx", "head"), None),
            P(("dp", "ctx", "head"), None),
            P(("dp", "ctx", "head"), None),
            P("dp", None),
            P("dp"),
            P("dp"),
        ),
        out_specs=(
            P(("dp", "ctx", "head"), None),
            P(("dp", "ctx"), "head"),
            P(("dp", "ctx"), "head"),
        ),
        check_vma=False,
    )
```

profile of v0, /device:TPU:32, one launch (start us, length us, event | category | flops | bytes accessed | tf_op | source)
XLA Modules:
  0.0 506.3 jit_solution(11946287480468813836)
XLA Ops:
  8.1 10.2 %all_to_all.95 = bf16[16,4,768]{2,0,1:T(8,128)(2,1)} all-to-all(bf16[16,4,768]{2,0,1:T(8,128)(2,1)S(1)} %bitcast.209), channel_id=1, replica_groups=mesh['dp'=2,'ctx'=32,'head'=4] {'head'}, dimensions={1} | all-to-all | bytes 196608 | tf_op jit(solution)/shard_map/all_to_all | solution.py:107
  19.2 8.8 %all_to_all.96 = bf16[16,4,768]{2,0,1:T(8,128)(2,1)} all-to-all(bf16[16,4,768]{2,0,1:T(8,128)(2,1)S(1)} %bitcast.210), channel_id=1, replica_groups=mesh['dp'=2,'ctx'=32,'head'=4] {'head'}, dimensions={1} | all-to-all | bytes 196608 | tf_op jit(solution)/shard_map/all_to_all | solution.py:106
  29.5 3.3 all-to-all-start.1
  39.8 4.8 all-to-all-start.3
  44.7 45.6 %all-gather = f32[32,64,6]{1,2,0:T(8,128)S(1)} all-gather(f32[1,64,6]{1,2,0:T(8,128)S(1)} %reshape.278), channel_id=1, replica_groups=mesh['dp'=2,'ctx'=32,'head'=4] {'ctx'}, dimensions={0}, use_global_device_ids=true | all-gather | bytes 50688 | tf_op jit(solution)/shard_map/all_gather | solution.py:123
  91.1 41.0 %all-gather.1 = f32[32,64,6]{1,2,0:T(8,128)S(1)} all-gather(f32[1,64,6]{1,2,0:T(8,128)S(1)} %reshape.280), channel_id=1, replica_groups=mesh['dp'=2,'ctx'=32,'head'=4] {'ctx'}, dimensions={0}, use_global_device_ids=true | all-gather | bytes 50688 | tf_op jit(solution)/shard_map/all_gather | solution.py:124
  132.8 7.7 %reshape.299 = bf16[8,256,6,128]{3,2,1,0:T(8,128)(2,1)} reshape(bf16[2048,768]{1,0:T(8,128)(2,1)} %all-gather.7.cloned.1.call-done) | data formatting | bytes 6291456 | tf_op jit(solution)/shard_map/reshape;reshape | solution.py:136
  140.5 3.0 copy.88
  143.5 34.0 %all-gather.5.cloned.1.call-done = bf16[2048,768]{1,0:T(8,128)(2,1)} async-done(((bf16[64,768]{1,0:T(8,128)(2,1)}), bf16[2048,768]{1,0:T(8,128)(2,1)}) %all-gather.5.cloned.1.call-update) | async-done | bytes 3145744 | tf_op jit(solution)/shard_map/all_gather | solution.py:119
  177.5 7.7 %reshape.298 = bf16[8,256,6,128]{3,2,1,0:T(8,128)(2,1)} reshape(bf16[2048,768]{1,0:T(8,128)(2,1)} %all-gather.5.cloned.1.call-done) | data formatting | bytes 6291456 | tf_op jit(solution)/shard_map/reshape;reshape | solution.py:136
  185.2 4.8 copy.86
  190.0 65.4 %while.15 = (s32[]{:T(128)}, f32[256,1,128]{0,2,1:T(8,128)S(1)}, f32[256,1,128]{0,2,1:T(8,128)S(1)}, f32[8,256,6,128]{3,1,2,0:T(8,128)}, bf16[8,256,6,128]{3,1,2...) while((s32[]{:T(128)}, f32[256,1,128]{0,2,1:T(8,128)S(1)}, ...), condition=%wide.region_5.6_spmd.clone, body=%wide.region_4.5_spmd.clone.sunk | while | flops 506823168 | bytes 10433308 | solution.py:164
  201.5 1.5 fusion.57
  209.7 1.5 fusion.57
  217.8 1.5 fusion.57
  234.2 1.5 fusion.57
  242.3 1.5 fusion.57
  250.5 1.5 fusion.57
  255.4 6.4 %copy.103 = f32[8,256,6,128]{3,2,1,0:T(8,128)S(1)} copy(f32[8,256,6,128]{3,1,2,0:T(8,128)} %get-tuple-element.82) | data formatting | bytes 12582912
  261.8 4.2 copy.119
  266.1 221.5 %reduce-scatter.4.cloned.1.call-done = f32[64,768]{1,0:T(8,128)} async-done(((f32[2048,768]{1,0:T(8,128)}), f32[64,768]{1,0:T(8,128)}) %reduce-scatter.4.cloned.1.call-update) | async-done | bytes 196624 | tf_op jit(solution)/shard_map/reduce_scatter | solution.py:165
  487.6 1.6 convert_element_type.24
  489.2 4.2 all-to-all-start.4
  494.8 4.3 all-to-all-done.4
  (189 shorter events, 70.0 us)
Async XLA Ops:
  7.2 125.6 %all-gather.7.cloned.1.call-start = ((), (), s32[]{:S(2)}) async-start(), calls=%async_computation.7 | async-start | bytes 3244032 | tf_op jit(solution)/shard_map/all_gather | solution.py:120
  18.3 159.2 %all-gather.5.cloned.1.call-start = ((), (), s32[]{:S(2)}) async-start(), calls=%async_computation.6 | async-start | bytes 3244032 | tf_op jit(solution)/shard_map/all_gather | solution.py:119
  29.5 10.4 %all-to-all-start.1 = ((f32[16,4,6]{0,2,1:T(8,128)}), f32[16,4,6]{0,2,1:T(8,128)S(1)}, u32[]{:S(2)}, u32[]{:S(2)}) async-start(f32[16,4,6]{0,2,1:T(8,128)} %all_to_all.74), calls=%async_computation.1 | async-start | bytes 32768 | tf_op jit(solution)/shard_map/all_to_all | solution.py:110
  39.8 51.1 %all-to-all-start.3 = ((f32[16,4,6]{0,2,1:T(8,128)}), f32[16,4,6]{0,2,1:T(8,128)S(1)}, u32[]{:S(2)}, u32[]{:S(2)}) async-start(f32[16,4,6]{0,2,1:T(8,128)} %all_to_all.82), calls=%async_computation.3 | async-start | bytes 32768 | tf_op jit(solution)/shard_map/all_to_all | solution.py:111
  44.6 443.0 %reduce-scatter.4.cloned.1.call-start = ((), (), s32[]{:S(2)}) async-start(), calls=%async_computation.8 | async-start | bytes 6488064 | tf_op jit(solution)/shard_map/reduce_scatter | solution.py:165
  185.2 4.8 copy-start
  185.2 4.8 copy-start.1
  190.0 0.7 copy-start.2
  195.2 3.0 copy-start.3
  198.2 0.7 copy-start.2
  203.4 3.0 copy-start.3
  206.4 0.7 copy-start.2
  211.5 3.0 copy-start.3
  214.6 0.7 copy-start.2
  219.7 3.0 copy-start.3
  222.7 0.7 copy-start.2
  227.9 3.0 copy-start.3
  230.9 0.7 copy-start.2
  236.0 3.0 copy-start.3
  239.1 0.7 copy-start.2
  244.2 3.1 copy-start.3
  247.3 0.7 copy-start.2
  252.4 3.0 copy-start.3
  489.2 10.0 %all-to-all-start.4 = ((bf16[4,16,768]{2,1,0:T(8,128)(2,1)}), bf16[4,16,768]{2,1,0:T(8,128)(2,1)S(1)}, u32[]{:S(2)}, u32[]{:S(2)}) async-start(bf16[4,16,768]{2,1,0:T(8,128)(2,1)} %bitcast.13), calls=%async_computation.4 | async-start | bytes 196608 | tf_op jit(solution)/shard_map/all_to_all | solution.py:173
Sparse Core Ops, SparseCore 0:
  18.4 79.8 all-gather.6
  100.9 76.5 all-gather.4
  266.2 221.3 reduce-scatter.3
where the time goes:
time: 510 us; the launch traced here: 506 us
  waiting for transfers between devices  260 us (51%)
  blocking collectives  106 us (21%)
  local copies, waits for them, and re-layouts  62.8 us (12%)
  matrix products  38.8 us (8%)
  between operations  13.8 us (3%)
  other arithmetic  12.6 us (2%)
  starting transfers between devices  12.3 us (2%)
    reduce_scatter x1, waiting for transfers between devices, local(): lax.psum_scatter(query_parts.reshape(queries_total, heads_loc * HEAD_DIM)...  222 us
    all_gather x1, blocking collectives, local(): lax.all_gather(norm_loc, 'ctx', axis=0, tiled=True)  45.6 us
    all_gather x1, blocking collectives, local(): lax.all_gather(delta_loc, 'ctx', axis=0, tiled=True)  41 us
    all_gather x1, waiting for transfers between devices, local(): lax.all_gather(query_loc, 'ctx', axis=0, tiled=True)  34 us
    unnamed x12, local copies, waits for them, and re-layouts  19.5 us
    dynamic_slice x40, local copies, waits for them, and re-layouts, local(): lax.scan(joint_step, (zeros_keys, zeros_keys), slab_blocks)  18.1 us
    another operation x2, local copies, waits for them, and re-layouts, as_blocks(): return values_in.reshape((block_count, block_rows) + values_in.shape[1:])  15.3 us
    dot_general x8, matrix products, pair_terms(): jnp.einsum('qhgd,khd->hgqk', query_grp, key_loc, preferred_element_type=j...  12 us
  transfers between devices with their start and end apart: 6, of which 3 were waited for; matrix products, arithmetic and copies ran while one was open for 4% of the time, Pallas kernels for 0%

commit v1 on v0

v1 whole, which is shorter than its diff:
```python
import functools
import math

import jax
import jax.numpy as jnp
from jax import lax
from jax.experimental import pallas as pl
from jax.experimental.pallas import tpu as pltpu
from jax.sharding import PartitionSpec as P

HEAD_DIM = 128
DISPATCH = 4
KCHUNK = 64
QCHUNK = 16
RING_X = 4
MESH = pl.DeviceIdType.MESH
F32 = jnp.float32
BF16 = jnp.bfloat16


def dot_nt(lhs, rhs):
    return lax.dot_general(lhs, rhs, (((1,), (1,)), ((), ())), preferred_element_type=F32)


def dot_nn(lhs, rhs):
    return lax.dot_general(lhs, rhs, (((1,), (0,)), ((), ())), preferred_element_type=F32)


def dot_tn(lhs, rhs):
    return lax.dot_general(lhs, rhs, (((0,), (0,)), ((), ())), preferred_element_type=F32)


def kernel(
    sizes,
    q_hbm,
    k_hbm,
    v_hbm,
    o_hbm,
    g_hbm,
    norm_hbm,
    table,
    key_order,
    query_order,
    dq_out,
    dk_out,
    dv_out,
    q_all,
    g_all,
    nd_all,
    k_all,
    v_all,
    q_own,
    o_own,
    g_own,
    norm_own,
    nd_own,
    nd_rows,
    bias,
    dq_acc,
    dq_send,
    dq_recv,
    part_k,
    part_v,
    chain_send,
    chain_recv,
    load_sem,
    plane_send,
    plane_recv,
    ring_send,
    ring_recv,
    chain_send_sem,
    chain_recv_sem,
    dq_send_sem,
    dq_recv_sem,
):
    size_z, size_x, size_y = sizes
    half = size_z // 2
    plane = size_x * size_y
    rows = plane * QCHUNK
    key_count = k_hbm.shape[0]
    heads_all = norm_hbm.shape[1]
    heads_loc = heads_all // size_y
    width = heads_loc * HEAD_DIM
    score_scale = 1.0 / math.sqrt(HEAD_DIM)
    log2e = math.log2(math.e)

    ctx = lax.axis_index("ctx")
    my_y = lax.axis_index("head")
    my_z = ctx // size_x
    my_x = ctx % size_x
    me = my_x * size_y + my_y
    my_rows = pl.ds(pl.multiple_of(me * QCHUNK, QCHUNK), QCHUNK)
    my_cols = pl.ds(pl.multiple_of(my_y * width, 128), width)

    def ring_z(offset):
        return (my_z + offset + size_z) % size_z

    def z_device(offset):
        return {"ctx": ring_z(offset) * size_x + my_x, "head": my_y}

    def plane_peer(dx, dy):
        px = (my_x + dx) % size_x
        py = (my_y + dy) % size_y
        return px, py, {"ctx": my_z * size_x + px, "head": py}

    peers = [(dx, dy) for dx in range(size_x) for dy in range(size_y) if dx or dy]
    peers.sort(key=lambda p: -(min(p[0], size_x - p[0]) + min(p[1], size_y - p[1])))

    own_k = k_all.at[my_z]
    own_v = v_all.at[my_z]
    loads = [
        pltpu.make_async_copy(k_hbm, own_k, load_sem.at[0]),
        pltpu.make_async_copy(v_hbm, own_v, load_sem.at[1]),
        pltpu.make_async_copy(g_hbm, g_own, load_sem.at[2]),
        pltpu.make_async_copy(o_hbm, o_own, load_sem.at[3]),
        pltpu.make_async_copy(norm_hbm, norm_own, load_sem.at[4]),
        pltpu.make_async_copy(q_hbm, q_own, load_sem.at[5]),
    ]
    for copy in loads:
        copy.start()

    barrier = pltpu.get_barrier_semaphore()
    for offset in (1, -1):
        pl.semaphore_signal(barrier, inc=1, device_id=z_device(offset), device_id_type=MESH)
    for dx, dy in peers:
        _, _, target = plane_peer(dx, dy)
        pl.semaphore_signal(barrier, inc=1, device_id=target, device_id_type=MESH)

    for copy in loads:
        copy.wait()

    lane = lax.broadcasted_iota(jnp.int32, (QCHUNK, 128), 1)
    tile = jnp.zeros((QCHUNK, 128), F32)
    for head in range(heads_all):
        cols = pl.ds(head * HEAD_DIM, HEAD_DIM)
        delta = jnp.sum(
            g_own[:, cols].astype(F32) * o_own[:, cols].astype(F32), axis=1, keepdims=True
        )
        tile = jnp.where(lane == heads_all + head, delta, tile)
    nd_own[...] = tile
    nd_own[:, 0:heads_all] = norm_own[...] * log2e

    pl.semaphore_wait(barrier, len(peers) + 2)

    def ring_copy(ref, way, step, index):
        slot = ring_z(-way * (step - 1))
        return pltpu.make_async_remote_copy(
            src_ref=ref.at[slot],
            dst_ref=ref.at[slot],
            send_sem=ring_send.at[index],
            recv_sem=ring_recv.at[index],
            device_id=z_device(way),
            device_id_type=MESH,
        )

    ring_plan = []
    for ref, way, steps in (
        (k_all, 1, half),
        (v_all, -1, half),
        (v_all, 1, half - 1),
        (k_all, -1, half - 1),
    ):
        ring_plan.append((ref, way, steps))
    ring = {}
    count = 0
    for step in range(1, half + 1):
        for line, (ref, way, steps) in enumerate(ring_plan):
            if step <= steps:
                ring[(line, step)] = ring_copy(ref, way, step, count)
                count += 1
    for line in range(4):
        if (line, 1) in ring:
            ring[(line, 1)].start()

    for slot, (dx, dy) in enumerate(peers):
        px, py, target = plane_peer(dx, dy)
        cols = pl.ds(pl.multiple_of(py * width, 128), width)
        for kind, (src, dst) in enumerate(
            ((nd_own, nd_all), (q_own.at[:, cols], q_all), (g_own.at[:, cols], g_all))
        ):
            pltpu.make_async_remote_copy(
                src_ref=src,
                dst_ref=dst.at[my_rows],
                send_sem=plane_send.at[kind],
                recv_sem=plane_recv.at[kind],
                device_id=target,
                device_id_type=MESH,
            ).start()
    pltpu.make_async_copy(nd_own, nd_all.at[my_rows], plane_recv.at[0]).start()
    pltpu.make_async_copy(q_own.at[:, my_cols], q_all.at[my_rows], plane_recv.at[1]).start()
    pltpu.make_async_copy(g_own.at[:, my_cols], g_all.at[my_rows], plane_recv.at[2]).start()

    qlane = lax.broadcasted_iota(jnp.int32, (1, rows), 1)
    qpos = jnp.zeros((1, rows), jnp.int32)
    for chunk in range(plane):
        qpos = jnp.where(qlane // QCHUNK == chunk, query_order[my_z * plane + chunk], qpos)
    offset = key_order.shape[0] * KCHUNK - query_order.shape[0] * QCHUNK
    qpos = offset + qpos * QCHUNK + qlane % QCHUNK
    low = jnp.zeros((1, rows), jnp.int32)
    high = jnp.zeros((1, rows), jnp.int32)
    for row in range(table.shape[0]):
        inside = (qpos >= table[row, 0]) & (qpos < table[row, 1])
        last = jnp.where(table[row, 4] != 0, jnp.minimum(table[row, 3], qpos + 1), table[row, 3])
        low = jnp.where(inside, table[row, 2], low)
        high = jnp.where(inside, last, high)
    krow = lax.broadcasted_iota(jnp.int32, (KCHUNK, rows), 0)
    dq_acc[...] = jnp.zeros_like(dq_acc)

    for step in range(2, half + 1):
        for line in range(4):
            if (line, step - 1) in ring:
                ring[(line, step - 1)].wait_recv()
            if (line, step) in ring:
                ring[(line, step)].start()

    for kind, dst in enumerate((nd_all, q_all, g_all)):
        pltpu.make_async_copy(dst, dst, plane_recv.at[kind]).wait()
    turned = nd_all[...].T
    nd_rows[...] = turned[0 : 2 * heads_all]

    order = [0, 1, -1, half]
    for distance in range(half - 1, 1, -1):
        order += [distance, -distance]

    def block_terms(index, dist):
        zb = ring_z(dist)
        first = (zb * size_x + my_x) * DISPATCH
        for part in range(DISPATCH):
            base = key_order[first + part] * KCHUNK
            ok = (krow >= low - base) & (krow < high - base)
            bias[pl.ds(part * KCHUNK, KCHUNK), :] = jnp.where(ok, jnp.inf, -jnp.inf).astype(F32)
        key_blk = k_all[zb]
        value_blk = v_all[zb]
        dk = jnp.zeros((key_count, HEAD_DIM), F32)
        dv = jnp.zeros((key_count, HEAD_DIM), F32)
        for head in range(heads_loc):
            cols = pl.ds(head * HEAD_DIM, HEAD_DIM)
            qh = q_all[:, cols]
            gh = g_all[:, cols]
            norm = nd_rows[pl.ds(my_y * heads_loc + head, 1), :]
            delta = nd_rows[pl.ds(heads_all + my_y * heads_loc + head, 1), :]
            scores = dot_nt(key_blk, qh)
            weights = jnp.exp2(jnp.minimum(scores * (score_scale * log2e) - norm, bias[...]))
            dprobs = dot_nt(value_blk, gh)
            dscore = (weights * (dprobs - delta)).astype(BF16)
            dv += dot_nn(weights.astype(BF16), gh)
            dk += dot_nn(dscore, qh)
            dq_acc[:, cols] += dot_tn(dscore, key_blk)
        part_k[index] = dk
        part_v[index] = dv

    lines = {("k", 1): half, ("v", -1): half, ("v", 1): half - 1, ("k", -1): half - 1}
    slots = {}
    for (kind, way), first_dist in lines.items():
        for dist in range(first_dist, 0, -1):
            slots[(kind, way, dist)] = len(slots)

    def chain_copy(kind, way, dist):
        slot = slots[(kind, way, dist)]
        return pltpu.make_async_remote_copy(
            src_ref=chain_send.at[slot],
            dst_ref=chain_recv.at[slot],
            send_sem=chain_send_sem.at[slot],
            recv_sem=chain_recv_sem.at[slot],
            device_id=z_device(way),
            device_id_type=MESH,
        )

    def chain_step(kind, way, dist):
        if (kind, way, dist) not in slots:
            return
        index = order.index(half if dist == half else way * dist)
        value = (part_k if kind == "k" else part_v)[index]
        if dist < lines[(kind, way)]:
            chain_copy(kind, way, dist + 1).wait_recv()
            value = value + chain_recv[slots[(kind, way, dist + 1)]].astype(F32)
        chain_send[slots[(kind, way, dist)]] = value.astype(BF16)
        chain_copy(kind, way, dist).start()

    def dist_at(index):
        later = index - 4
        far = half - 1 - later // 2
        return jnp.where(
            index == 0,
            0,
            jnp.where(
                index == 1,
                1,
                jnp.where(
                    index == 2,
                    -1,
                    jnp.where(index == 3, half, jnp.where(later % 2 == 0, far, -far)),
                ),
            ),
        )

    def block_step(index, carry):
        @pl.when(index == 3)
        def _():
            for line in range(4):
                if ring_plan[line][2] == half:
                    ring[(line, half)].wait_recv()

        block_terms(index, dist_at(index))

        for at in range(3, size_z):
            dist = order[at]

            @pl.when(index == at)
            def _(dist=dist):
                if dist == half:
                    chain_step("k", 1, half)
                    chain_step("v", -1, half)
                elif dist > 0:
                    chain_step("v", 1, dist)
                else:
                    chain_step("k", -1, -dist)
                    chain_step("k", 1, -dist)
                    chain_step("v", -1, -dist)

        return carry

    lax.fori_loop(0, size_z, block_step, 0)

    dq_send[...] = dq_acc[...].astype(BF16)
    for dx, dy in peers:
        px, py, target = plane_peer(dx, dy)
        peer_rows = pl.ds(pl.multiple_of((px * size_y + py) * QCHUNK, QCHUNK), QCHUNK)
        pltpu.make_async_remote_copy(
            src_ref=dq_send.at[peer_rows],
            dst_ref=dq_recv.at[my_x, :, my_cols],
            send_sem=dq_send_sem,
            recv_sem=dq_recv_sem,
            device_id=target,
            device_id_type=MESH,
        ).start()
    pltpu.make_async_copy(
        dq_send.at[my_rows], dq_recv.at[my_x, :, my_cols], dq_recv_sem
    ).start()

    chain_step("v", 1, 1)
    chain_step("k", -1, 1)
    chain_step("k", 1, 1)
    chain_step("v", -1, 1)

    pltpu.make_async_copy(dq_recv, dq_recv, dq_recv_sem).wait()
    total = dq_recv[0].astype(F32)
    for other in range(1, size_x):
        total = total + dq_recv[other].astype(F32)
    dq_out[...] = (total * score_scale).astype(BF16)

    for kind, part, out, scale in (("v", part_v, dv_out, 1.0), ("k", part_k, dk_out, score_scale)):
        value = part[0]
        for way in (1, -1):
            if (kind, way, 1) in slots:
                chain_copy(kind, way, 1).wait_recv()
                value = value + chain_recv[slots[(kind, way, 1)]].astype(F32)
        out[...] = (value * scale).astype(BF16)

    for copy in ring.values():
        copy.wait_send()
    for key in slots:
        chain_copy(*key).wait_send()
    sent = pl.ds(0, len(peers) * QCHUNK)
    for kind, dst in enumerate((nd_all, q_all, g_all)):
        pltpu.make_async_copy(dst.at[sent], dst.at[sent], plane_send.at[kind]).wait()
    pltpu.make_async_copy(dq_send.at[sent], dq_send.at[sent], dq_send_sem).wait()


def local(
    sizes,
    query_rows,
    key_rows,
    value_rows,
    output_rows,
    grad_out,
    log_norm,
    mask_table,
    key_order,
    query_order,
):
    size_z, size_x, size_y = sizes
    half = size_z // 2
    rows = size_x * size_y * QCHUNK
    key_count = key_rows.shape[0]
    own, columns = query_rows.shape
    heads_all = log_norm.shape[1]
    width = columns // size_y
    chain = 2 * (2 * half - 1)
    hbm = pl.BlockSpec(memory_space=pl.ANY)
    smem = pl.BlockSpec(memory_space=pltpu.SMEM)
    vmem = pl.BlockSpec(memory_space=pltpu.VMEM)
    dma = pltpu.SemaphoreType.DMA
    return pl.pallas_call(
        functools.partial(kernel, sizes),
        out_shape=(
            jax.ShapeDtypeStruct(query_rows.shape, BF16),
            jax.ShapeDtypeStruct(key_rows.shape, BF16),
            jax.ShapeDtypeStruct(value_rows.shape, BF16),
        ),
        in_specs=[hbm] * 6 + [smem] * 3,
        out_specs=(vmem, vmem, vmem),
        scratch_shapes=[
            pltpu.VMEM((rows, width), BF16),
            pltpu.VMEM((rows, width), BF16),
            pltpu.VMEM((rows, 128), F32),
            pltpu.VMEM((size_z, key_count, HEAD_DIM), BF16),
            pltpu.VMEM((size_z, key_count, HEAD_DIM), BF16),
            pltpu.VMEM((own, columns), BF16),
            pltpu.VMEM((own, columns), BF16),
            pltpu.VMEM((own, columns), BF16),
            pltpu.VMEM((own, heads_all), F32),
            pltpu.VMEM((own, 128), F32),
            pltpu.VMEM((2 * heads_all, rows), F32),
            pltpu.VMEM((key_count, rows), F32),
            pltpu.VMEM((rows, width), F32),
            pltpu.VMEM((rows, width), BF16),
            pltpu.VMEM((size_x, own, columns), BF16),
            pltpu.VMEM((size_z, key_count, HEAD_DIM), F32),
            pltpu.VMEM((size_z, key_count, HEAD_DIM), F32),
            pltpu.VMEM((chain, key_count, HEAD_DIM), BF16),
            pltpu.VMEM((chain, key_count, HEAD_DIM), BF16),
            dma((6,)),
            dma((3,)),
            dma((3,)),
            dma((chain,)),
            dma((chain,)),
            dma((chain,)),
            dma((chain,)),
            dma,
            dma,
        ],
        compiler_params=pltpu.CompilerParams(
            collective_id=0, has_side_effects=True, vmem_limit_bytes=32 * 1024 * 1024
        ),
    )(
        query_rows,
        key_rows,
        value_rows,
        output_rows,
        grad_out,
        log_norm,
        mask_table,
        key_order,
        query_order,
    )


def solution(mesh, ring_x=RING_X):
    sizes = (mesh.shape["ctx"] // ring_x, ring_x, mesh.shape["head"])
    return jax.shard_map(
        functools.partial(local, sizes),
        mesh=mesh,
        in_specs=(
            P(("dp", "ctx", "head"), None),
            P(("dp", "ctx"), "head"),
            P(("dp", "ctx"), "head"),
            P(("dp", "ctx", "head"), None),
            P(("dp", "ctx", "head"), None),
            P(("dp", "ctx", "head"), None),
            P("dp", None),
            P("dp"),
            P("dp"),
        ),
        out_specs=(
            P(("dp", "ctx", "head"), None),
            P(("dp", "ctx"), "head"),
            P(("dp", "ctx"), "head"),
        ),
        check_vma=False,
    )
```

time: 510 us -> 56.5 us (0.11)
  waiting for transfers between devices: 260 us -> 0 us
  blocking collectives: 106 us -> 0 us
  local copies, waits for them, and re-layouts: 62.8 us -> 7.04 us
  Pallas kernels: 0 us -> 48.4 us
  matrix products: 38.8 us -> 0 us
  between operations: 13.8 us -> 0.68 us
  other arithmetic: 12.6 us -> 0 us
  starting transfers between devices: 12.3 us -> 0 us
    reduce_scatter x1 -> x0, waiting for transfers between devices: 222 us -> none  [local(): lax.psum_scatter(query_parts.reshape(queries_total, heads_loc * HEAD_DIM)...]
    all_gather x2 -> x0, blocking collectives: 86.6 us -> none  [the longest x1 45.6 us: local(): lax.all_gather(norm_loc, 'ctx', axis=0, tiled=True)]
    pallas_call x0 -> x1, Pallas kernels: none -> 48.4 us  [local(): pl.pallas_call(functools.partial(kernel, sizes), out_shape=(jax.ShapeDtyp...]
    dot_general x40 -> x0, matrix products: 38.8 us -> none  [the longest x8 12 us: pair_terms(): jnp.einsum('qhgd,khd->hgqk', query_grp, key_loc, preferred_element_type=j...]
    all_gather x2 -> x0, waiting for transfers between devices: 34 us -> none  [the longest x1 34 us: local(): lax.all_gather(query_loc, 'ctx', axis=0, tiled=True)]
    all_to_all x2 -> x0, blocking collectives: 19 us -> none  [the longest x1 10.2 us: local(): lax.all_to_all(grad_out, 'head', split_axis=1, concat_axis=0, tiled=True)]
    dynamic_slice x40 -> x0, local copies, waits for them, and re-layouts: 18.1 us -> none  [local(): lax.scan(joint_step, (zeros_keys, zeros_keys), slab_blocks)]
    another operation x2 -> x0, local copies, waits for them, and re-layouts: 15.3 us -> none  [as_blocks(): return values_in.reshape((block_count, block_rows) + values_in.shape[1:])]
  transfers between devices with their start and end apart: 6 -> 0, of which waited for: 3 -> 0; matrix products, arithmetic and copies ran while one was open for 4% -> 0% of each run, Pallas kernels for 0% -> 0%
where the time goes in v1:
time: 56.5 us; the launch traced here: 56.1 us
  Pallas kernels  48.4 us (86%)
  local copies, waits for them, and re-layouts  7.04 us (12%)
  between operations  0.68 us (1%)
    pallas_call x1, Pallas kernels, local(): pl.pallas_call(functools.partial(kernel, sizes), out_shape=(jax.ShapeDtyp...  48.4 us
    unnamed x20, local copies, waits for them, and re-layouts  7.04 us

profile of v1, /device:TPU:32, one launch (start us, length us, event | category | flops | bytes accessed | tf_op | source)
XLA Modules:
  0.0 56.1 jit_solution(1473456960998243626)
XLA Ops:
  0.6 0.0 copy-start.7
  0.6 0.0 copy-start.6
  0.7 0.0 copy-start.5
  0.7 0.8 %copy.12.table = s32[16,5]{1,0:T(8,128)S(1)} copy(s32[16,5]{0,1:T(8,128)} %param.15) | data formatting | bytes 640 | tf_op args[6]
  1.4 0.0 copy-done.7
  1.4 0.0 copy-done.6
  1.4 0.0 copy-done.5
  1.5 0.0 copy-start
  1.5 0.9 %copy-done = bf16[16,3072]{1,0:T(8,128)(2,1)S(1)} copy-done((bf16[16,3072]{1,0:T(8,128)(2,1)S(1)}, bf16[16,3072]{1,0:T(8,128)(2,1)}, u32[]{:S(2)}) %copy-start) | copy-done | bytes 98328
  2.3 0.0 copy-start.1
  2.4 0.9 %copy-done.1 = bf16[16,3072]{1,0:T(8,128)(2,1)S(1)} copy-done((bf16[16,3072]{1,0:T(8,128)(2,1)S(1)}, bf16[16,3072]{1,0:T(8,128)(2,1)}, u32[]{:S(2)}) %copy-start.1) | copy-done | bytes 98328
  3.2 0.0 copy-start.2
  3.2 0.9 %copy-done.2 = bf16[16,3072]{1,0:T(8,128)(2,1)S(1)} copy-done((bf16[16,3072]{1,0:T(8,128)(2,1)S(1)}, bf16[16,3072]{1,0:T(8,128)(2,1)}, u32[]{:S(2)}) %copy-start.2) | copy-done | bytes 98328
  4.1 0.0 copy-start.3
  4.1 0.8 %copy-done.3 = bf16[256,128]{1,0:T(8,128)(2,1)S(1)} copy-done((bf16[256,128]{1,0:T(8,128)(2,1)S(1)}, bf16[256,128]{1,0:T(8,128)(2,1)}, u32[]{:S(2)}) %copy-start.3) | copy-done | bytes 65560
  5.0 0.0 copy-start.4
  5.0 0.8 %copy-done.4 = bf16[256,128]{1,0:T(8,128)(2,1)S(1)} copy-done((bf16[256,128]{1,0:T(8,128)(2,1)S(1)}, bf16[256,128]{1,0:T(8,128)(2,1)}, u32[]{:S(2)}) %copy-start.4) | copy-done | bytes 65560
  5.8 48.4 %shard_map.112 = (bf16[16,3072]{1,0:T(8,128)(2,1)S(1)}, bf16[256,128]{1,0:T(8,128)(2,1)S(1)}, bf16[256,128]{1,0:T(8,128)(2,1)S(1)}) custom-call(bf16[16,3072]{1,0:T(8,128)(2,1)S(1)} %copy-done, bf16[256,128]{1,0:T(8,128)(2,1)S(1)} %copy-done.3, bf16[256,128]{1,0:T(8,128)(2,1)S(1)} %copy-done.4, bf16[16,3072]{1,0:T(8,128)(2,1)S(1)} %copy-done.1, ...), custom_call_target="tpu_custom_call" | custom-call | tf_op jit(solution)/shard_map/pallas_call | solution.py:394
  54.2 0.6 %copy.16 = bf16[16,3072]{1,0:T(8,128)(2,1)} copy(bf16[16,3072]{1,0:T(8,128)(2,1)S(1)} %get-tuple-element.6) | data formatting | bytes 196608
  54.9 0.6 %copy.17 = bf16[256,128]{1,0:T(8,128)(2,1)} copy(bf16[256,128]{1,0:T(8,128)(2,1)S(1)} %get-tuple-element.7) | data formatting | bytes 131072
  55.5 0.6 %copy.18 = bf16[256,128]{1,0:T(8,128)(2,1)} copy(bf16[256,128]{1,0:T(8,128)(2,1)S(1)} %get-tuple-element.8) | data formatting | bytes 131072
Async XLA Ops:
  0.6 0.8 %copy-start.7 = (s32[128]{0:T(128)S(1)}, s32[128]{0:T(128)}, u32[]{:S(2)}) copy-start(s32[128]{0:T(128)} %query_order.1) | copy-start | bytes 1540
  0.6 0.8 %copy-start.6 = (s32[128]{0:T(128)S(1)}, s32[128]{0:T(128)}, u32[]{:S(2)}) copy-start(s32[128]{0:T(128)} %key_order.1) | copy-start | bytes 1540
  0.7 0.8 %copy-start.5 = (f32[16,24]{1,0:T(8,128)S(1)}, f32[16,24]{1,0:T(8,128)}, u32[]{:S(2)}) copy-start(f32[16,24]{1,0:T(8,128)} %norm_hbm.1) | copy-start | bytes 4612
  1.5 0.9 %copy-start = (bf16[16,3072]{1,0:T(8,128)(2,1)S(1)}, bf16[16,3072]{1,0:T(8,128)(2,1)}, u32[]{:S(2)}) copy-start(bf16[16,3072]{1,0:T(8,128)(2,1)} %q_hbm.1) | copy-start | bytes 294916
  2.3 0.9 %copy-start.1 = (bf16[16,3072]{1,0:T(8,128)(2,1)S(1)}, bf16[16,3072]{1,0:T(8,128)(2,1)}, u32[]{:S(2)}) copy-start(bf16[16,3072]{1,0:T(8,128)(2,1)} %o_hbm.1) | copy-start | bytes 294916
  3.2 0.9 %copy-start.2 = (bf16[16,3072]{1,0:T(8,128)(2,1)S(1)}, bf16[16,3072]{1,0:T(8,128)(2,1)}, u32[]{:S(2)}) copy-start(bf16[16,3072]{1,0:T(8,128)(2,1)} %g_hbm.1) | copy-start | bytes 294916
  4.1 0.8 %copy-start.3 = (bf16[256,128]{1,0:T(8,128)(2,1)S(1)}, bf16[256,128]{1,0:T(8,128)(2,1)}, u32[]{:S(2)}) copy-start(bf16[256,128]{1,0:T(8,128)(2,1)} %k_hbm.1) | copy-start | bytes 196612
  5.0 0.8 %copy-start.4 = (bf16[256,128]{1,0:T(8,128)(2,1)S(1)}, bf16[256,128]{1,0:T(8,128)(2,1)}, u32[]{:S(2)}) copy-start(bf16[256,128]{1,0:T(8,128)(2,1)} %v_hbm.1) | copy-start | bytes 196612

commit v2 on v1

v2 whole, which is shorter than its diff:
```python
import functools
import math

import jax
import jax.numpy as jnp
from jax import lax
from jax.experimental import pallas as pl
from jax.experimental.pallas import tpu as pltpu
from jax.sharding import PartitionSpec as P

HEAD_DIM = 128
DISPATCH = 4
KCHUNK = 64
QCHUNK = 16
RING_X = 4
MESH = pl.DeviceIdType.MESH
F32 = jnp.float32
BF16 = jnp.bfloat16


def dot_nt(lhs, rhs):
    return lax.dot_general(lhs, rhs, (((1,), (1,)), ((), ())), preferred_element_type=F32)


def dot_nn(lhs, rhs):
    return lax.dot_general(lhs, rhs, (((1,), (0,)), ((), ())), preferred_element_type=F32)


def kernel(
    sizes,
    q_hbm,
    k_hbm,
    v_hbm,
    o_hbm,
    g_hbm,
    norm_hbm,
    table_hbm,
    key_order_hbm,
    query_order_hbm,
    dq_out,
    dk_out,
    dv_out,
    qg_all,
    nd_all,
    k_all,
    v_all,
    q_own,
    o_own,
    g_own,
    norm_own,
    nd_own,
    nd_rows,
    table,
    key_order,
    query_order,
    bias,
    dq_acc,
    dq_send,
    dq_recv,
    part_k,
    part_v,
    chain_send,
    chain_recv,
    dq_stage,
    dk_stage,
    dv_stage,
    load_sem,
    own_sem,
    relay_sem,
    qg_send_sem,
    nd_send_sem,
    qg_recv_sem,
    nd_recv_sem,
    ring_send,
    ring_recv,
    chain_send_sem,
    chain_recv_sem,
    dq_send_sem,
    dq_recv_sem,
    store_sem,
):
    size_z, size_x, size_y = sizes
    half = size_z // 2
    plane = size_x * size_y
    rows = plane * QCHUNK
    key_count = k_hbm.shape[0]
    heads_all = norm_hbm.shape[1]
    heads_loc = heads_all // size_y
    width = heads_loc * HEAD_DIM
    score_scale = 1.0 / math.sqrt(HEAD_DIM)
    log2e = math.log2(math.e)

    ctx = lax.axis_index("ctx")
    my_y = lax.axis_index("head")
    my_z = ctx // size_x
    my_x = ctx % size_x
    me = my_x * size_y + my_y
    my_rows = pl.ds(pl.multiple_of(me * QCHUNK, QCHUNK), QCHUNK)
    my_cols = pl.ds(pl.multiple_of(my_y * width, 128), width)

    def ring_z(offset):
        return (my_z + offset + size_z) % size_z

    def device(dz, dx, dy):
        return {
            "ctx": ring_z(dz) * size_x + (my_x + dx + size_x) % size_x,
            "head": (my_y + dy + size_y) % size_y,
        }

    def z_device(offset):
        return device(offset, 0, 0)

    def chunk_rows(sx, sy):
        chunk = (my_x + sx + size_x) % size_x * size_y + (my_y + sy + size_y) % size_y
        return pl.ds(pl.multiple_of(chunk * QCHUNK, QCHUNK), QCHUNK)

    own_k = k_all.at[my_z]
    own_v = v_all.at[my_z]
    loads = [
        pltpu.make_async_copy(k_hbm, own_k, load_sem.at[0]),
        pltpu.make_async_copy(v_hbm, own_v, load_sem.at[1]),
        pltpu.make_async_copy(g_hbm, g_own, load_sem.at[2]),
        pltpu.make_async_copy(o_hbm, o_own, load_sem.at[3]),
        pltpu.make_async_copy(norm_hbm, norm_own, load_sem.at[4]),
        pltpu.make_async_copy(q_hbm, q_own, load_sem.at[5]),
        pltpu.make_async_copy(table_hbm, table, load_sem.at[6]),
        pltpu.make_async_copy(key_order_hbm, key_order, load_sem.at[7]),
        pltpu.make_async_copy(query_order_hbm, query_order, load_sem.at[8]),
    ]
    for copy in loads:
        copy.start()

    barrier = pltpu.get_barrier_semaphore()
    neighbours = [(1, 0, 0), (-1, 0, 0), (0, 1, 0), (0, -1, 0), (0, 0, 1), (0, 0, -1)]
    for neighbour in neighbours:
        pl.semaphore_signal(
            barrier, inc=1, device_id=device(*neighbour), device_id_type=MESH
        )

    for copy in loads:
        copy.wait()

    lane = lax.broadcasted_iota(jnp.int32, (QCHUNK, 128), 1)
    tile = jnp.zeros((QCHUNK, 128), F32)
    for head in range(heads_all):
        cols = pl.ds(head * HEAD_DIM, HEAD_DIM)
        delta = jnp.sum(
            g_own[:, cols].astype(F32) * o_own[:, cols].astype(F32), axis=1, keepdims=True
        )
        tile = jnp.where(lane == heads_all + head, delta, tile)
    nd_own[...] = tile
    nd_own[:, 0:heads_all] = norm_own[...] * log2e

    pl.semaphore_wait(barrier, len(neighbours))

    for way in (1, -1):
        pl.semaphore_signal(
            relay_sem, inc=1, device_id=device(0, 0, way), device_id_type=MESH
        )

    def ring_copy(ref, way, step, index):
        slot = ring_z(-way * (step - 1))
        return pltpu.make_async_remote_copy(
            src_ref=ref.at[slot],
            dst_ref=ref.at[slot],
            send_sem=ring_send.at[index],
            recv_sem=ring_recv.at[index],
            device_id=z_device(way),
            device_id_type=MESH,
        )

    ring_plan = []
    for ref, way, steps in (
        (k_all, 1, half),
        (v_all, -1, half),
        (v_all, 1, half - 1),
        (k_all, -1, half - 1),
    ):
        ring_plan.append((ref, way, steps))
    ring = {}
    count = 0
    for step in range(1, half + 1):
        for line, (ref, way, steps) in enumerate(ring_plan):
            if step <= steps:
                ring[(line, step)] = ring_copy(ref, way, step, count)
                count += 1
    for line in range(4):
        if (line, 1) in ring:
            ring[(line, 1)].start()

    def slot_of(sx, sy):
        return (sx + 2 * size_x) % size_x * size_y + (sy + 2 * size_y) % size_y

    def plane_copy(src, dst, sends, receives, tx, ty, sx, sy):
        slot = slot_of(sx - tx, sy - ty)
        pltpu.make_async_remote_copy(
            src_ref=src,
            dst_ref=dst,
            send_sem=sends,
            recv_sem=receives.at[slot],
            device_id=device(0, tx, ty),
            device_id_type=MESH,
        ).start()

    def send_own(tx, ty):
        group = (my_y + ty + size_y) % size_y
        cols = pl.ds(pl.multiple_of(group * width, 128), width)
        for part, src in enumerate((q_own, g_own)):
            plane_copy(
                src.at[:, cols],
                qg_all.at[my_rows, pl.ds(part * width, width)],
                qg_send_sem,
                qg_recv_sem,
                tx,
                ty,
                0,
                0,
            )
        plane_copy(nd_own, nd_all.at[my_rows], nd_send_sem, nd_recv_sem, tx, ty, 0, 0)

    def wait_chunk(sx, sy):
        at = chunk_rows(sx, sy)
        slot = slot_of(sx, sy)
        pltpu.make_async_copy(qg_all.at[at], qg_all.at[at], qg_recv_sem.at[slot]).wait()
        pltpu.make_async_copy(nd_all.at[at], nd_all.at[at], nd_recv_sem.at[slot]).wait()

    def forward(sx, sy, way):
        at = chunk_rows(sx, sy)
        plane_copy(qg_all.at[at], qg_all.at[at], qg_send_sem, qg_recv_sem, way, 0, sx, sy)
        plane_copy(nd_all.at[at], nd_all.at[at], nd_send_sem, nd_recv_sem, way, 0, sx, sy)

    def ring_step(step):
        for line in range(4):
            if (line, step - 1) in ring:
                ring[(line, step - 1)].wait_recv()
            if (line, step) in ring:
                ring[(line, step)].start()

    send_own(0, 1)
    send_own(0, -1)
    send_own(1, 0)
    send_own(-1, 0)
    own_copies = [
        pltpu.make_async_copy(nd_own, nd_all.at[my_rows], own_sem.at[0]),
        pltpu.make_async_copy(
            q_own.at[:, my_cols], qg_all.at[my_rows, pl.ds(0, width)], own_sem.at[1]
        ),
        pltpu.make_async_copy(
            g_own.at[:, my_cols], qg_all.at[my_rows, pl.ds(width, width)], own_sem.at[2]
        ),
    ]
    for copy in own_copies:
        copy.start()
    pl.semaphore_wait(relay_sem, 2)
    send_own(0, 2)

    qlane = lax.broadcasted_iota(jnp.int32, (1, rows), 1)
    qpos = jnp.zeros((1, rows), jnp.int32)
    for chunk in range(plane):
        qpos = jnp.where(qlane // QCHUNK == chunk, query_order[my_z * plane + chunk], qpos)
    offset = key_order.shape[0] * KCHUNK - query_order.shape[0] * QCHUNK
    qpos = offset + qpos * QCHUNK + qlane % QCHUNK
    low = jnp.zeros((1, rows), jnp.int32)
    high = jnp.zeros((1, rows), jnp.int32)
    for row in range(table.shape[1]):
        inside = (qpos >= table[0, row]) & (qpos < table[1, row])
        last = jnp.where(table[4, row] != 0, jnp.minimum(table[3, row], qpos + 1), table[3, row])
        low = jnp.where(inside, table[2, row], low)
        high = jnp.where(inside, last, high)
    krow = lax.broadcasted_iota(jnp.int32, (KCHUNK, rows), 0)
    dq_acc[...] = jnp.zeros_like(dq_acc)

    for sy in (-1, 1):
        wait_chunk(0, sy)
        forward(0, sy, 1)
        forward(0, sy, -1)
    if half > 1:
        ring_step(2)
    wait_chunk(0, 2)
    forward(0, 2, 1)
    forward(0, 2, -1)
    for sy in (0, 1):
        wait_chunk(-1, sy)
        forward(-1, sy, 1)
    for sy in (-1, 2):
        wait_chunk(1, sy)
        forward(1, sy, -1)
    for step in range(3, half):
        ring_step(step)
    for sy in (0, 1):
        wait_chunk(1, sy)
    for sy in (-1, 2):
        wait_chunk(-1, sy)
    for sy in range(size_y):
        wait_chunk(2, sy)
    for copy in own_copies:
        copy.wait()
    turned = nd_all[...].T
    nd_rows[...] = turned[0 : 2 * heads_all]

    order = [0, half - 1, 1 - half, half]
    for distance in range(half - 2, 0, -1):
        order += [distance, -distance]

    def by_head(first):
        return jnp.concatenate(
            [qg_all[:, pl.ds(first + head * HEAD_DIM, HEAD_DIM)] for head in range(heads_loc)],
            axis=0,
        )

    def block_terms(index, dist):
        zb = ring_z(dist)
        first = (zb * size_x + my_x) * DISPATCH
        for part in range(DISPATCH):
            base = key_order[first + part] * KCHUNK
            ok = (krow >= low - base) & (krow < high - base)
            bias[pl.ds(part * KCHUNK, KCHUNK), :] = jnp.where(ok, jnp.inf, -jnp.inf).astype(F32)
        key_blk = k_all[zb]
        value_blk = v_all[zb]
        weights_low = []
        dscores = []
        for head in range(heads_loc):
            cols = pl.ds(head * HEAD_DIM, HEAD_DIM)
            norm = nd_rows[pl.ds(my_y * heads_loc + head, 1), :]
            delta = nd_rows[pl.ds(heads_all + my_y * heads_loc + head, 1), :]
            scores = dot_nt(key_blk, qg_all[:, cols])
            weights = jnp.exp2(jnp.minimum(scores * (score_scale * log2e) - norm, bias[...]))
            dprobs = dot_nt(value_blk, qg_all[:, pl.ds(width + head * HEAD_DIM, HEAD_DIM)])
            weights_low.append(weights.astype(BF16))
            dscores.append((weights * (dprobs - delta)).astype(BF16))
        part_v[index] = dot_nn(jnp.concatenate(weights_low, axis=1), by_head(width))
        part_k[index] = dot_nn(jnp.concatenate(dscores, axis=1), by_head(0))
        key_turned = key_blk.T
        for head in range(heads_loc):
            dq_acc[:, pl.ds(head * rows, rows)] += dot_nn(key_turned, dscores[head])

    slots = {}
    for dist in range(half - 1, 0, -1):
        for way in (1, -1):
            for kind in ("k", "v"):
                slots[(kind, way, dist)] = len(slots)
    far = {("k", 1): len(slots), ("v", -1): len(slots) + 1}

    def slot_copy(slot, dz):
        return pltpu.make_async_remote_copy(
            src_ref=chain_send.at[slot],
            dst_ref=chain_recv.at[slot],
            send_sem=chain_send_sem.at[slot],
            recv_sem=chain_recv_sem.at[slot],
            device_id=z_device(dz),
            device_id_type=MESH,
        )

    def chain_copy(kind, way, dist):
        return slot_copy(slots[(kind, way, dist)], way)

    def far_copy(kind, way):
        return slot_copy(far[(kind, way)], way * (half - 1))

    def chain_step(kind, way, dist):
        value = (part_k if kind == "k" else part_v)[order.index(way * dist)]
        if dist < half - 1:
            chain_copy(kind, way, dist + 1).wait_recv()
            value = value + chain_recv[slots[(kind, way, dist + 1)]].astype(F32)
        if dist == 1 and (kind, way) in far:
            far_copy(kind, way).wait_recv()
            value = value + chain_recv[far[(kind, way)]].astype(F32)
        chain_send[slots[(kind, way, dist)]] = value.astype(BF16)
        chain_copy(kind, way, dist).start()

    def far_step():
        for (kind, way), slot in far.items():
            value = (part_k if kind == "k" else part_v)[order.index(half)]
            chain_send[slot] = value.astype(BF16)
            far_copy(kind, way).start()

    def dist_at(index):
        later = index - 4
        near = half - 2 - later // 2
        return jnp.where(
            index == 0,
            0,
            jnp.where(
                index == 1,
                half - 1,
                jnp.where(
                    index == 2,
                    1 - half,
                    jnp.where(index == 3, half, jnp.where(later % 2 == 0, near, -near)),
                ),
            ),
        )

    def block_step(index, carry):
        @pl.when(index == 1)
        def _():
            ring_step(half)

        @pl.when(index == 3)
        def _():
            ring_step(half + 1)

        block_terms(index, dist_at(index))

        for at in range(1, size_z):
            dist = order[at]
            if dist == half or abs(dist) > 1:

                @pl.when(index == at)
                def _(dist=dist):
                    if dist == half:
                        far_step()
                    else:
                        way = 1 if dist > 0 else -1
                        chain_step("k", way, abs(dist))
                        chain_step("v", way, abs(dist))

        return carry

    lax.fori_loop(0, size_z, block_step, 0)

    peers = [(dx, dy) for dx in range(size_x) for dy in range(size_y) if dx or dy]
    peers.sort(key=lambda p: -(min(p[0], size_x - p[0]) + min(p[1], size_y - p[1])))
    for head in range(heads_loc):
        turned = dq_acc[:, pl.ds(head * rows, rows)].T
        dq_send[:, pl.ds(head * HEAD_DIM, HEAD_DIM)] = turned.astype(BF16)
    for dx, dy in peers:
        pltpu.make_async_remote_copy(
            src_ref=dq_send.at[chunk_rows(dx, dy)],
            dst_ref=dq_recv.at[my_x, :, my_cols],
            send_sem=dq_send_sem,
            recv_sem=dq_recv_sem,
            device_id=device(0, dx, dy),
            device_id_type=MESH,
        ).start()
    pltpu.make_async_copy(
        dq_send.at[my_rows], dq_recv.at[my_x, :, my_cols], dq_recv_sem
    ).start()

    for way in (1, -1):
        for kind in ("k", "v"):
            chain_step(kind, way, 1)

    pltpu.make_async_copy(dq_recv, dq_recv, dq_recv_sem).wait()
    total = dq_recv[0].astype(F32)
    for other in range(1, size_x):
        total = total + dq_recv[other].astype(F32)
    dq_stage[...] = (total * score_scale).astype(BF16)
    stores = [pltpu.make_async_copy(dq_stage, dq_out, store_sem.at[0])]
    stores[0].start()

    for kind, part, stage, out, scale in (
        ("v", part_v, dv_stage, dv_out, 1.0),
        ("k", part_k, dk_stage, dk_out, score_scale),
    ):
        value = part[0]
        for way in (1, -1):
            chain_copy(kind, way, 1).wait_recv()
            value = value + chain_recv[slots[(kind, way, 1)]].astype(F32)
        stage[...] = (value * scale).astype(BF16)
        stores.append(pltpu.make_async_copy(stage, out, store_sem.at[len(stores)]))
        stores[-1].start()

    for copy in ring.values():
        copy.wait_send()
    for key in slots:
        chain_copy(*key).wait_send()
    for key in far:
        far_copy(*key).wait_send()
    sent = pl.ds(0, len(peers) * QCHUNK)
    pltpu.make_async_copy(qg_all.at[sent], qg_all.at[sent], qg_send_sem).wait()
    pltpu.make_async_copy(nd_all.at[sent], nd_all.at[sent], nd_send_sem).wait()
    pltpu.make_async_copy(dq_send.at[sent], dq_send.at[sent], dq_send_sem).wait()
    for copy in stores:
        copy.wait()


def local(
    sizes,
    query_rows,
    key_rows,
    value_rows,
    output_rows,
    grad_out,
    log_norm,
    mask_table,
    key_order,
    query_order,
):
    size_z, size_x, size_y = sizes
    half = size_z // 2
    rows = size_x * size_y * QCHUNK
    key_count = key_rows.shape[0]
    own, columns = query_rows.shape
    heads_all = log_norm.shape[1]
    width = columns // size_y
    chain = 2 * (2 * half - 1)
    hbm = pl.BlockSpec(memory_space=pltpu.HBM)
    dma = pltpu.SemaphoreType.DMA
    return pl.pallas_call(
        functools.partial(kernel, sizes),
        out_shape=(
            jax.ShapeDtypeStruct(query_rows.shape, BF16),
            jax.ShapeDtypeStruct(key_rows.shape, BF16),
            jax.ShapeDtypeStruct(value_rows.shape, BF16),
        ),
        in_specs=[hbm] * 9,
        out_specs=(hbm, hbm, hbm),
        scratch_shapes=[
            pltpu.VMEM((rows, 2 * width), BF16),
            pltpu.VMEM((rows, 128), F32),
            pltpu.VMEM((size_z, key_count, HEAD_DIM), BF16),
            pltpu.VMEM((size_z, key_count, HEAD_DIM), BF16),
            pltpu.VMEM((own, columns), BF16),
            pltpu.VMEM((own, columns), BF16),
            pltpu.VMEM((own, columns), BF16),
            pltpu.VMEM((own, heads_all), F32),
            pltpu.VMEM((own, 128), F32),
            pltpu.VMEM((2 * heads_all, rows), F32),
            pltpu.SMEM(mask_table.shape[::-1], jnp.int32),
            pltpu.SMEM(key_order.shape, jnp.int32),
            pltpu.SMEM(query_order.shape, jnp.int32),
            pltpu.VMEM((key_count, rows), F32),
            pltpu.VMEM((HEAD_DIM, width // HEAD_DIM * rows), F32),
            pltpu.VMEM((rows, width), BF16),
            pltpu.VMEM((size_x, own, columns), BF16),
            pltpu.VMEM((size_z, key_count, HEAD_DIM), F32),
            pltpu.VMEM((size_z, key_count, HEAD_DIM), F32),
            pltpu.VMEM((chain, key_count, HEAD_DIM), BF16),
            pltpu.VMEM((chain, key_count, HEAD_DIM), BF16),
            pltpu.VMEM((own, columns), BF16),
            pltpu.VMEM((key_count, HEAD_DIM), BF16),
            pltpu.VMEM((key_count, HEAD_DIM), BF16),
            dma((9,)),
            dma((3,)),
            pltpu.SemaphoreType.REGULAR,
            dma,
            dma,
            dma((size_x * size_y,)),
            dma((size_x * size_y,)),
            dma((chain,)),
            dma((chain,)),
            dma((chain,)),
            dma((chain,)),
            dma,
            dma,
            dma((3,)),
        ],
        compiler_params=pltpu.CompilerParams(
            collective_id=0, has_side_effects=True, vmem_limit_bytes=60 * 1024 * 1024
        ),
    )(
        query_rows,
        key_rows,
        value_rows,
        output_rows,
        grad_out,
        log_norm,
        mask_table.T,
        key_order,
        query_order,
    )


def solution(mesh, ring_x=RING_X):
    sizes = (mesh.shape["ctx"] // ring_x, ring_x, mesh.shape["head"])
    return jax.shard_map(
        functools.partial(local, sizes),
        mesh=mesh,
        in_specs=(
            P(("dp", "ctx", "head"), None),
            P(("dp", "ctx"), "head"),
            P(("dp", "ctx"), "head"),
            P(("dp", "ctx", "head"), None),
            P(("dp", "ctx", "head"), None),
            P(("dp", "ctx", "head"), None),
            P("dp", None),
            P("dp"),
            P("dp"),
        ),
        out_specs=(
            P(("dp", "ctx", "head"), None),
            P(("dp", "ctx"), "head"),
            P(("dp", "ctx"), "head"),
        ),
        check_vma=False,
    )
```

time: 56.5 us -> 45.7 us (0.81)
  Pallas kernels: 48.4 us -> 41.3 us
  local copies, waits for them, and re-layouts: 7.04 us -> 3.07 us
    pallas_call x1, Pallas kernels: 48.4 us -> 41.3 us  [local(): pl.pallas_call(functools.partial(kernel, sizes), out_shape=(jax.ShapeDtyp...]
    unnamed x20 -> x7, local copies, waits for them, and re-layouts: 7.04 us -> 3.07 us
where the time goes in v2:
time: 45.7 us; the launch traced here: 45 us
  Pallas kernels  41.3 us (90%)
  local copies, waits for them, and re-layouts  3.07 us (7%)
  between operations  0.65 us (1%)
    pallas_call x1, Pallas kernels, local(): pl.pallas_call(functools.partial(kernel, sizes), out_shape=(jax.ShapeDtyp...  41.3 us
    unnamed x7, local copies, waits for them, and re-layouts  3.07 us

profile of v2, /device:TPU:32, one launch (start us, length us, event | category | flops | bytes accessed | tf_op | source)
XLA Modules:
  0.0 45.0 jit_solution(7803232034275949978)
XLA Ops:
  0.6 41.3 %shard_map.112 = (bf16[16,3072]{1,0:T(8,128)(2,1)}, bf16[256,128]{1,0:T(8,128)(2,1)}, bf16[256,128]{1,0:T(8,128)(2,1)}) custom-call(bf16[16,3072]{1,0:T(8,128)(2,1)} %q_hbm.1, bf16[256,128]{1,0:T(8,128)(2,1)} %k_hbm.1, bf16[256,128]{1,0:T(8,128)(2,1)} %v_hbm.1, bf16[16,3072]{1,0:T(8,128)(2,1)} %o_hbm.1, bf16[16,3072]{1,0:T(8,128)(2,1)} %g_hbm.1, ...), custom_call_target="tpu_custom_call" | custom-call | tf_op jit(solution)/shard_map/pallas_call | solution.py:500
  42.0 0.0 copy-start.1
  42.0 1.6 %copy.15 = bf16[16,3072]{1,0:T(8,128)(2,1)} copy(bf16[16,3072]{1,0:T(8,128)(2,1)} %get-tuple-element.6) | data formatting | bytes 196608
  43.6 0.0 copy-done.1
  43.6 0.0 copy-start
  43.6 0.6 %copy.16 = bf16[256,128]{1,0:T(8,128)(2,1)} copy(bf16[256,128]{1,0:T(8,128)(2,1)S(1)} %copy-done.1) | data formatting | bytes 131072
  44.2 0.2 copy-done
  44.4 0.6 %copy.17 = bf16[256,128]{1,0:T(8,128)(2,1)} copy(bf16[256,128]{1,0:T(8,128)(2,1)S(1)} %copy-done) | data formatting | bytes 131072
Async XLA Ops:
  42.0 1.6 %copy-start.1 = (bf16[256,128]{1,0:T(8,128)(2,1)S(1)}, bf16[256,128]{1,0:T(8,128)(2,1)}, u32[]{:S(2)}) copy-start(bf16[256,128]{1,0:T(8,128)(2,1)} %get-tuple-element.7) | copy-start | bytes 196612
  43.6 0.9 %copy-start = (bf16[256,128]{1,0:T(8,128)(2,1)S(1)}, bf16[256,128]{1,0:T(8,128)(2,1)}, u32[]{:S(2)}) copy-start(bf16[256,128]{1,0:T(8,128)(2,1)} %get-tuple-element.8) | copy-start | bytes 196612

commit v3 on v2

--- a/solution.py
+++ b/solution.py
@@ -37,9 +37,11 @@
     table_hbm,
     key_order_hbm,
     query_order_hbm,
-    dq_out,
-    dk_out,
-    dv_out,
+    dq_recv,
+    own_k,
+    own_v,
+    recv_k,
+    recv_v,
     qg_all,
     nd_all,
     k_all,
@@ -56,14 +58,10 @@
     bias,
     dq_acc,
     dq_send,
-    dq_recv,
     part_k,
     part_v,
     chain_send,
     chain_recv,
-    dq_stage,
-    dk_stage,
-    dv_stage,
     load_sem,
     own_sem,
     relay_sem,
@@ -114,11 +112,16 @@
         chunk = (my_x + sx + size_x) % size_x * size_y + (my_y + sy + size_y) % size_y
         return pl.ds(pl.multiple_of(chunk * QCHUNK, QCHUNK), QCHUNK)
 
-    own_k = k_all.at[my_z]
-    own_v = v_all.at[my_z]
+    barrier = pltpu.get_barrier_semaphore()
+    neighbours = [(1, 0, 0), (-1, 0, 0), (0, 1, 0), (0, -1, 0), (0, 0, 1), (0, 0, -1)]
+    for neighbour in neighbours:
+        pl.semaphore_signal(
+            barrier, inc=1, device_id=device(*neighbour), device_id_type=MESH
+        )
+
     loads = [
-        pltpu.make_async_copy(k_hbm, own_k, load_sem.at[0]),
-        pltpu.make_async_copy(v_hbm, own_v, load_sem.at[1]),
+        pltpu.make_async_copy(k_hbm, k_all.at[my_z], load_sem.at[0]),
+        pltpu.make_async_copy(v_hbm, v_all.at[my_z], load_sem.at[1]),
         pltpu.make_async_copy(g_hbm, g_own, load_sem.at[2]),
         pltpu.make_async_copy(o_hbm, o_own, load_sem.at[3]),
         pltpu.make_async_copy(norm_hbm, norm_own, load_sem.at[4]),
@@ -130,38 +133,13 @@
     for copy in loads:
         copy.start()
 
-    barrier = pltpu.get_barrier_semaphore()
-    neighbours = [(1, 0, 0), (-1, 0, 0), (0, 1, 0), (0, -1, 0), (0, 0, 1), (0, 0, -1)]
-    for neighbour in neighbours:
-        pl.semaphore_signal(
-            barrier, inc=1, device_id=device(*neighbour), device_id_type=MESH
-        )
-
-    for copy in loads:
-        copy.wait()
-
-    lane = lax.broadcasted_iota(jnp.int32, (QCHUNK, 128), 1)
-    tile = jnp.zeros((QCHUNK, 128), F32)
-    for head in range(heads_all):
-        cols = pl.ds(head * HEAD_DIM, HEAD_DIM)
-        delta = jnp.sum(
-            g_own[:, cols].astype(F32) * o_own[:, cols].astype(F32), axis=1, keepdims=True
-        )
-        tile = jnp.where(lane == heads_all + head, delta, tile)
-    nd_own[...] = tile
-    nd_own[:, 0:heads_all] = norm_own[...] * log2e
-
     pl.semaphore_wait(barrier, len(neighbours))
-
-    for way in (1, -1):
-        pl.semaphore_signal(
-            relay_sem, inc=1, device_id=device(0, 0, way), device_id_type=MESH
-        )
 
     def ring_copy(ref, way, step, index):
         slot = ring_z(-way * (step - 1))
+        src = ref.at[slot] if step > 1 else (k_hbm if ref is k_all else v_hbm)
         return pltpu.make_async_remote_copy(
-            src_ref=ref.at[slot],
+            src_ref=src,
             dst_ref=ref.at[slot],
             send_sem=ring_send.at[index],
             recv_sem=ring_recv.at[index],
@@ -188,6 +166,25 @@
         if (line, 1) in ring:
             ring[(line, 1)].start()
 
+    for way in (1, -1):
+        pl.semaphore_signal(
+            relay_sem, inc=1, device_id=device(0, 0, way), device_id_type=MESH
+        )
+
+    for copy in loads:
+        copy.wait()
+
+    lane = lax.broadcasted_iota(jnp.int32, (QCHUNK, 128), 1)
+    tile = jnp.zeros((QCHUNK, 128), F32)
+    for head in range(heads_all):
+        cols = pl.ds(head * HEAD_DIM, HEAD_DIM)
+        delta = jnp.sum(
+            g_own[:, cols].astype(F32) * o_own[:, cols].astype(F32), axis=1, keepdims=True
+        )
+        tile = jnp.where(lane == heads_all + head, delta, tile)
+    nd_own[...] = tile
+    nd_own[:, 0:heads_all] = norm_own[...] * log2e
+
     def slot_of(sx, sy):
         return (sx + 2 * size_x) % size_x * size_y + (sy + 2 * size_y) % size_y
 
@@ -270,22 +267,23 @@
     krow = lax.broadcasted_iota(jnp.int32, (KCHUNK, rows), 0)
     dq_acc[...] = jnp.zeros_like(dq_acc)
 
+    ring_step(2)
     for sy in (-1, 1):
         wait_chunk(0, sy)
         forward(0, sy, 1)
         forward(0, sy, -1)
-    if half > 1:
-        ring_step(2)
     wait_chunk(0, 2)
     forward(0, 2, 1)
     forward(0, 2, -1)
+    if half > 2:
+        ring_step(3)
     for sy in (0, 1):
         wait_chunk(-1, sy)
         forward(-1, sy, 1)
     for sy in (-1, 2):
         wait_chunk(1, sy)
         forward(1, sy, -1)
-    for step in range(3, half):
+    for step in range(4, half + 1):
         ring_step(step)
     for sy in (0, 1):
         wait_chunk(1, sy)
@@ -298,8 +296,8 @@
     turned = nd_all[...].T
     nd_rows[...] = turned[0 : 2 * heads_all]
 
-    order = [0, half - 1, 1 - half, half]
-    for distance in range(half - 2, 0, -1):
+    order = [0, half]
+    for distance in range(half - 1, 0, -1):
         order += [distance, -distance]
 
     def by_head(first):
@@ -334,90 +332,77 @@
         for head in range(heads_loc):
             dq_acc[:, pl.ds(head * rows, rows)] += dot_nn(key_turned, dscores[head])
 
+    lines = {("k", 1): half, ("v", -1): half, ("v", 1): half - 1, ("k", -1): half - 1}
     slots = {}
-    for dist in range(half - 1, 0, -1):
-        for way in (1, -1):
-            for kind in ("k", "v"):
-                slots[(kind, way, dist)] = len(slots)
-    far = {("k", 1): len(slots), ("v", -1): len(slots) + 1}
-
-    def slot_copy(slot, dz):
+    for (kind, way), first_dist in lines.items():
+        for dist in range(first_dist, 0, -1):
+            slots[(kind, way, dist)] = len(slots)
+
+    def chain_copy(kind, way, dist):
+        slot = slots[(kind, way, dist)]
+        dst = chain_recv.at[slot]
+        if dist == 1:
+            dst = (recv_k if kind == "k" else recv_v).at[0 if way == 1 else 1]
         return pltpu.make_async_remote_copy(
             src_ref=chain_send.at[slot],
-            dst_ref=chain_recv.at[slot],
+            dst_ref=dst,
             send_sem=chain_send_sem.at[slot],
             recv_sem=chain_recv_sem.at[slot],
-            device_id=z_device(dz),
+            device_id=z_device(way),
             device_id_type=MESH,
         )
 
-    def chain_copy(kind, way, dist):
-        return slot_copy(slots[(kind, way, dist)], way)
-
-    def far_copy(kind, way):
-        return slot_copy(far[(kind, way)], way * (half - 1))
-
     def chain_step(kind, way, dist):
-        value = (part_k if kind == "k" else part_v)[order.index(way * dist)]
-        if dist < half - 1:
+        index = order.index(half if dist == half else way * dist)
+        value = (part_k if kind == "k" else part_v)[index]
+        if dist < lines[(kind, way)]:
             chain_copy(kind, way, dist + 1).wait_recv()
             value = value + chain_recv[slots[(kind, way, dist + 1)]].astype(F32)
-        if dist == 1 and (kind, way) in far:
-            far_copy(kind, way).wait_recv()
-            value = value + chain_recv[far[(kind, way)]].astype(F32)
         chain_send[slots[(kind, way, dist)]] = value.astype(BF16)
         chain_copy(kind, way, dist).start()
 
-    def far_step():
-        for (kind, way), slot in far.items():
-            value = (part_k if kind == "k" else part_v)[order.index(half)]
-            chain_send[slot] = value.astype(BF16)
-            far_copy(kind, way).start()
+    events = {at: [] for at in range(size_z + 1)}
+    for (kind, way), first_dist in lines.items():
+        for dist in range(first_dist, 0, -1):
+            at = order.index(half if dist == half else way * dist)
+            if first_dist == half and dist < half:
+                at = 4 + 3 * (half - 1 - dist)
+            elif dist < half - 1:
+                at = 5 + 3 * (half - 2 - dist) + (way < 0)
+            events[min(at, size_z) if dist > 1 else size_z].append((kind, way, dist))
+    for listed in events.values():
+        listed.sort(key=lambda e: lines[(e[0], e[1])] - half)
 
     def dist_at(index):
-        later = index - 4
-        near = half - 2 - later // 2
-        return jnp.where(
-            index == 0,
-            0,
-            jnp.where(
-                index == 1,
-                half - 1,
-                jnp.where(
-                    index == 2,
-                    1 - half,
-                    jnp.where(index == 3, half, jnp.where(later % 2 == 0, near, -near)),
-                ),
-            ),
-        )
+        near = half - index // 2
+        paired = jnp.where(index % 2 == 0, near, -near)
+        return jnp.where(index == 0, 0, jnp.where(index == 1, half, paired))
 
     def block_step(index, carry):
         @pl.when(index == 1)
         def _():
-            ring_step(half)
-
-        @pl.when(index == 3)
-        def _():
             ring_step(half + 1)
 
         block_terms(index, dist_at(index))
 
         for at in range(1, size_z):
-            dist = order[at]
-            if dist == half or abs(dist) > 1:
+            if events[at]:
 
                 @pl.when(index == at)
-                def _(dist=dist):
-                    if dist == half:
-                        far_step()
-                    else:
-                        way = 1 if dist > 0 else -1
-                        chain_step("k", way, abs(dist))
-                        chain_step("v", way, abs(dist))
+                def _(at=at):
+                    for event in events[at]:
+                        chain_step(*event)
 
         return carry
 
     lax.fori_loop(0, size_z, block_step, 0)
+
+    stores = [
+        pltpu.make_async_copy(part_k.at[0], own_k, store_sem.at[0]),
+        pltpu.make_async_copy(part_v.at[0], own_v, store_sem.at[1]),
+    ]
+    for copy in stores:
+        copy.start()
 
     peers = [(dx, dy) for dx in range(size_x) for dy in range(size_y) if dx or dy]
     peers.sort(key=lambda p: -(min(p[0], size_x - p[0]) + min(p[1], size_y - p[1])))
@@ -437,42 +422,53 @@
         dq_send.at[my_rows], dq_recv.at[my_x, :, my_cols], dq_recv_sem
     ).start()
 
-    for way in (1, -1):
-        for kind in ("k", "v"):
-            chain_step(kind, way, 1)
+    for event in events[size_z]:
+        chain_step(*event)
 
     pltpu.make_async_copy(dq_recv, dq_recv, dq_recv_sem).wait()
-    total = dq_recv[0].astype(F32)
-    for other in range(1, size_x):
-        total = total + dq_recv[other].astype(F32)
-    dq_stage[...] = (total * score_scale).astype(BF16)
-    stores = [pltpu.make_async_copy(dq_stage, dq_out, store_sem.at[0])]
-    stores[0].start()
-
-    for kind, part, stage, out, scale in (
-        ("v", part_v, dv_stage, dv_out, 1.0),
-        ("k", part_k, dk_stage, dk_out, score_scale),
-    ):
-        value = part[0]
-        for way in (1, -1):
-            chain_copy(kind, way, 1).wait_recv()
-            value = value + chain_recv[slots[(kind, way, 1)]].astype(F32)
-        stage[...] = (value * scale).astype(BF16)
-        stores.append(pltpu.make_async_copy(stage, out, store_sem.at[len(stores)]))
-        stores[-1].start()
+    for key in slots:
+        if key[2] == 1:
+            chain_copy(*key).wait_recv()
 
     for copy in ring.values():
         copy.wait_send()
     for key in slots:
         chain_copy(*key).wait_send()
-    for key in far:
-        far_copy(*key).wait_send()
     sent = pl.ds(0, len(peers) * QCHUNK)
     pltpu.make_async_copy(qg_all.at[sent], qg_all.at[sent], qg_send_sem).wait()
     pltpu.make_async_copy(nd_all.at[sent], nd_all.at[sent], nd_send_sem).wait()
     pltpu.make_async_copy(dq_send.at[sent], dq_send.at[sent], dq_send_sem).wait()
     for copy in stores:
         copy.wait()
+
+
+def add_up_kernel(dq_recv, own_k, own_v, recv_k, recv_v, dq_out, dk_out, dv_out):
+    score_scale = 1.0 / math.sqrt(HEAD_DIM)
+    total = dq_recv[0].astype(F32)
+    for other in range(1, dq_recv.shape[0]):
+        total = total + dq_recv[other].astype(F32)
+    dq_out[...] = (total * score_scale).astype(BF16)
+    total = own_k[...] + recv_k[0].astype(F32) + recv_k[1].astype(F32)
+    dk_out[...] = (total * score_scale).astype(BF16)
+    total = own_v[...] + recv_v[0].astype(F32) + recv_v[1].astype(F32)
+    dv_out[...] = total.astype(BF16)
+
+
+def add_up(terms):
+    vmem = pl.BlockSpec(memory_space=pltpu.VMEM)
+    dq_recv, own_k, own_v = terms[:3]
+    return pl.pallas_call(
+        add_up_kernel,
+        out_shape=(
+            jax.ShapeDtypeStruct(dq_recv.shape[1:], BF16),
+            jax.ShapeDtypeStruct(own_k.shape, BF16),
+            jax.ShapeDtypeStruct(own_v.shape, BF16),
+        ),
+        in_specs=[vmem] * 5,
+        out_specs=(vmem,) * 3,
+        name="add_up",
+        compiler_params=pltpu.CompilerParams(vmem_limit_bytes=60 * 1024 * 1024),
+    )(*terms)
 
 
 def local(
@@ -497,15 +493,17 @@
     chain = 2 * (2 * half - 1)
     hbm = pl.BlockSpec(memory_space=pltpu.HBM)
     dma = pltpu.SemaphoreType.DMA
-    return pl.pallas_call(
+    terms = pl.pallas_call(
         functools.partial(kernel, sizes),
         out_shape=(
-            jax.ShapeDtypeStruct(query_rows.shape, BF16),
-            jax.ShapeDtypeStruct(key_rows.shape, BF16),
-            jax.ShapeDtypeStruct(value_rows.shape, BF16),
+            jax.ShapeDtypeStruct((size_x,) + query_rows.shape, BF16),
+            jax.ShapeDtypeStruct(key_rows.shape, F32),
+            jax.ShapeDtypeStruct(value_rows.shape, F32),
+            jax.ShapeDtypeStruct((2,) + key_rows.shape, BF16),
+            jax.ShapeDtypeStruct((2,) + value_rows.shape, BF16),
         ),
         in_specs=[hbm] * 9,
-        out_specs=(hbm, hbm, hbm),
+        out_specs=(hbm,) * 5,
         scratch_shapes=[
             pltpu.VMEM((rows, 2 * width), BF16),
             pltpu.VMEM((rows, 128), F32),
@@ -523,14 +521,10 @@
             pltpu.VMEM((key_count, rows), F32),
             pltpu.VMEM((HEAD_DIM, width // HEAD_DIM * rows), F32),
             pltpu.VMEM((rows, width), BF16),
-            pltpu.VMEM((size_x, own, columns), BF16),
             pltpu.VMEM((size_z, key_count, HEAD_DIM), F32),
             pltpu.VMEM((size_z, key_count, HEAD_DIM), F32),
             pltpu.VMEM((chain, key_count, HEAD_DIM), BF16),
             pltpu.VMEM((chain, key_count, HEAD_DIM), BF16),
-            pltpu.VMEM((own, columns), BF16),
-            pltpu.VMEM((key_count, HEAD_DIM), BF16),
-            pltpu.VMEM((key_count, HEAD_DIM), BF16),
             dma((9,)),
             dma((3,)),
             pltpu.SemaphoreType.REGULAR,
@@ -544,7 +538,7 @@
             dma((chain,)),
             dma,
             dma,
-            dma((3,)),
+            dma((2,)),
         ],
         compiler_params=pltpu.CompilerParams(
             collective_id=0, has_side_effects=True, vmem_limit_bytes=60 * 1024 * 1024
@@ -560,6 +554,7 @@
         key_order,
         query_order,
     )
+    return add_up(terms)
 
 
 def solution(mesh, ring_x=RING_X):

time: 45.7 us -> 43.4 us (0.950)
  local copies, waits for them, and re-layouts: 3.07 us -> 0 us
  Pallas kernels: 41.3 us -> 42 us
    unnamed x7 -> x0, local copies, waits for them, and re-layouts: 3.07 us -> none
    pallas_call x0 -> x1, Pallas kernels: none -> 1.94 us  [add_up(): pl.pallas_call(add_up_kernel, out_shape=(jax.ShapeDtypeStruct(dq_recv.sha...]
    pallas_call x1, Pallas kernels: 41.3 us -> 40 us  [local(): pl.pallas_call(functools.partial(kernel, sizes), out_shape=(jax.ShapeDtyp...]
where the time goes in v3:
time: 43.4 us; the launch traced here: 42.6 us
  Pallas kernels  42 us (97%)
  between operations  0.64 us (1%)
    pallas_call x1, Pallas kernels, local(): pl.pallas_call(functools.partial(kernel, sizes), out_shape=(jax.ShapeDtyp...  40 us
    pallas_call x1, Pallas kernels, add_up(): pl.pallas_call(add_up_kernel, out_shape=(jax.ShapeDtypeStruct(dq_recv.sha...  1.94 us

profile of v3, /device:TPU:32, one launch (start us, length us, event | category | flops | bytes accessed | tf_op | source)
XLA Modules:
  0.0 42.6 jit_solution(1498692656113735747)
XLA Ops:
  0.6 40.0 %shard_map.112 = (bf16[4,16,3072]{2,1,0:T(8,128)(2,1)}, f32[256,128]{1,0:T(8,128)}, f32[256,128]{1,0:T(8,128)}, bf16[2,256,128]{2,1,0:T(8,128)(2,1)}, bf16[2,256,128]{2,1,0:T(8,128)(2,1)}) custom-call(bf16[16,3072]{1,0:T(8,128)(2,1)} %q_hbm.1, bf16[256,128]{1,0:T(8,128)(2,1)} %k_hbm.1, bf16[256,128]{1,0:T(8,128)(2,1)} %v_hbm.1, bf16[16,3072]{1,0:T(8,128)(2,1)} %o_hbm.1, ...), custom_call_target="tpu_custom_call" | custom-call | tf_op jit(solution)/shard_map/pallas_call | solution.py:496
  40.7 1.9 %add_up.1 = (bf16[16,3072]{1,0:T(8,128)(2,1)}, bf16[256,128]{1,0:T(8,128)(2,1)}, bf16[256,128]{1,0:T(8,128)(2,1)}) custom-call(bf16[4,16,3072]{2,1,0:T(8,128)(2,1)} %get-tuple-element.8.dq_recv, f32[256,128]{1,0:T(8,128)} %get-tuple-element.9.own_k, f32[256,128]{1,0:T(8,128)} %get-tuple-element.10.own_v, bf16[2,256,128]{2,1,0:T(8,128)(2,1)} %get-tuple-element.11.recv_k, ...), custom_call_target="tpu_custom_call" | custom-call | tf_op jit(solution)/shard_map/add_up/pallas_call | solution.py:460

commit v4 on v3

--- a/solution.py
+++ b/solution.py
@@ -46,7 +46,6 @@
     nd_all,
     k_all,
     v_all,
-    q_own,
     o_own,
     g_own,
     norm_own,
@@ -65,6 +64,7 @@
     load_sem,
     own_sem,
     relay_sem,
+    relay_x_sem,
     qg_send_sem,
     nd_send_sem,
     qg_recv_sem,
@@ -119,20 +119,6 @@
             barrier, inc=1, device_id=device(*neighbour), device_id_type=MESH
         )
 
-    loads = [
-        pltpu.make_async_copy(k_hbm, k_all.at[my_z], load_sem.at[0]),
-        pltpu.make_async_copy(v_hbm, v_all.at[my_z], load_sem.at[1]),
-        pltpu.make_async_copy(g_hbm, g_own, load_sem.at[2]),
-        pltpu.make_async_copy(o_hbm, o_own, load_sem.at[3]),
-        pltpu.make_async_copy(norm_hbm, norm_own, load_sem.at[4]),
-        pltpu.make_async_copy(q_hbm, q_own, load_sem.at[5]),
-        pltpu.make_async_copy(table_hbm, table, load_sem.at[6]),
-        pltpu.make_async_copy(key_order_hbm, key_order, load_sem.at[7]),
-        pltpu.make_async_copy(query_order_hbm, query_order, load_sem.at[8]),
-    ]
-    for copy in loads:
-        copy.start()
-
     pl.semaphore_wait(barrier, len(neighbours))
 
     def ring_copy(ref, way, step, index):
@@ -171,19 +157,18 @@
             relay_sem, inc=1, device_id=device(0, 0, way), device_id_type=MESH
         )
 
+    loads = [
+        pltpu.make_async_copy(k_hbm, k_all.at[my_z], load_sem.at[0]),
+        pltpu.make_async_copy(v_hbm, v_all.at[my_z], load_sem.at[1]),
+        pltpu.make_async_copy(g_hbm, g_own, load_sem.at[2]),
+        pltpu.make_async_copy(o_hbm, o_own, load_sem.at[3]),
+        pltpu.make_async_copy(norm_hbm, norm_own, load_sem.at[4]),
+        pltpu.make_async_copy(table_hbm, table, load_sem.at[5]),
+        pltpu.make_async_copy(key_order_hbm, key_order, load_sem.at[6]),
+        pltpu.make_async_copy(query_order_hbm, query_order, load_sem.at[7]),
+    ]
     for copy in loads:
-        copy.wait()
-
-    lane = lax.broadcasted_iota(jnp.int32, (QCHUNK, 128), 1)
-    tile = jnp.zeros((QCHUNK, 128), F32)
-    for head in range(heads_all):
-        cols = pl.ds(head * HEAD_DIM, HEAD_DIM)
-        delta = jnp.sum(
-            g_own[:, cols].astype(F32) * o_own[:, cols].astype(F32), axis=1, keepdims=True
-        )
-        tile = jnp.where(lane == heads_all + head, delta, tile)
-    nd_own[...] = tile
-    nd_own[:, 0:heads_all] = norm_own[...] * log2e
+        copy.start()
 
     def slot_of(sx, sy):
         return (sx + 2 * size_x) % size_x * size_y + (sy + 2 * size_y) % size_y
@@ -199,10 +184,10 @@
             device_id_type=MESH,
         ).start()
 
-    def send_own(tx, ty):
+    def send_rows(tx, ty):
         group = (my_y + ty + size_y) % size_y
         cols = pl.ds(pl.multiple_of(group * width, 128), width)
-        for part, src in enumerate((q_own, g_own)):
+        for part, src in enumerate((q_hbm, g_hbm)):
             plane_copy(
                 src.at[:, cols],
                 qg_all.at[my_rows, pl.ds(part * width, width)],
@@ -213,6 +198,8 @@
                 0,
                 0,
             )
+
+    def send_nd(tx, ty):
         plane_copy(nd_own, nd_all.at[my_rows], nd_send_sem, nd_recv_sem, tx, ty, 0, 0)
 
     def wait_chunk(sx, sy):
@@ -233,24 +220,60 @@
             if (line, step) in ring:
                 ring[(line, step)].start()
 
-    send_own(0, 1)
-    send_own(0, -1)
-    send_own(1, 0)
-    send_own(-1, 0)
+    beside = ((0, 1), (0, -1), (1, 0), (-1, 0))
+    for peer in beside:
+        send_rows(*peer)
     own_copies = [
-        pltpu.make_async_copy(nd_own, nd_all.at[my_rows], own_sem.at[0]),
         pltpu.make_async_copy(
-            q_own.at[:, my_cols], qg_all.at[my_rows, pl.ds(0, width)], own_sem.at[1]
+            q_hbm.at[:, my_cols], qg_all.at[my_rows, pl.ds(0, width)], own_sem.at[1]
         ),
         pltpu.make_async_copy(
-            g_own.at[:, my_cols], qg_all.at[my_rows, pl.ds(width, width)], own_sem.at[2]
+            g_hbm.at[:, my_cols], qg_all.at[my_rows, pl.ds(width, width)], own_sem.at[2]
         ),
     ]
     for copy in own_copies:
         copy.start()
+
+    for copy in loads:
+        copy.wait()
+
+    lane = lax.broadcasted_iota(jnp.int32, (QCHUNK, 128), 1)
+    tile = jnp.zeros((QCHUNK, 128), F32)
+    for head in range(heads_all):
+        cols = pl.ds(head * HEAD_DIM, HEAD_DIM)
+        delta = jnp.sum(
+            g_own[:, cols].astype(F32) * o_own[:, cols].astype(F32), axis=1, keepdims=True
+        )
+        tile = jnp.where(lane == heads_all + head, delta, tile)
+    nd_own[...] = tile
+    nd_own[:, 0:heads_all] = norm_own[...] * log2e
+
+    for peer in beside:
+        send_nd(*peer)
+    own_copies.append(pltpu.make_async_copy(nd_own, nd_all.at[my_rows], own_sem.at[0]))
+    own_copies[-1].start()
     pl.semaphore_wait(relay_sem, 2)
-    send_own(0, 2)
-
+    for way in (1, -1):
+        pl.semaphore_signal(
+            relay_x_sem, inc=1, device_id=device(0, way, 0), device_id_type=MESH
+        )
+    send_rows(0, 2)
+    send_nd(0, 2)
+
+    pl.semaphore_wait(relay_x_sem, 2)
+    for tx in (1, -1):
+        for ty in (1, -1, 2):
+            send_rows(tx, ty)
+            send_nd(tx, ty)
+    ring_step(2)
+    if half > 2:
+        ring_step(3)
+    for sy in (0, 1):
+        wait_chunk(-1, sy)
+        forward(-1, sy, 1)
+    for sy in (-1, 2):
+        wait_chunk(1, sy)
+        forward(1, sy, -1)
     qlane = lax.broadcasted_iota(jnp.int32, (1, rows), 1)
     qpos = jnp.zeros((1, rows), jnp.int32)
     for chunk in range(plane):
@@ -267,24 +290,10 @@
     krow = lax.broadcasted_iota(jnp.int32, (KCHUNK, rows), 0)
     dq_acc[...] = jnp.zeros_like(dq_acc)
 
-    ring_step(2)
-    for sy in (-1, 1):
-        wait_chunk(0, sy)
-        forward(0, sy, 1)
-        forward(0, sy, -1)
-    wait_chunk(0, 2)
-    forward(0, 2, 1)
-    forward(0, 2, -1)
-    if half > 2:
-        ring_step(3)
-    for sy in (0, 1):
-        wait_chunk(-1, sy)
-        forward(-1, sy, 1)
-    for sy in (-1, 2):
-        wait_chunk(1, sy)
-        forward(1, sy, -1)
     for step in range(4, half + 1):
         ring_step(step)
+    for sy in (1, 2, -1):
+        wait_chunk(0, sy)
     for sy in (0, 1):
         wait_chunk(1, sy)
     for sy in (-1, 2):
@@ -348,30 +357,29 @@
             dst_ref=dst,
             send_sem=chain_send_sem.at[slot],
             recv_sem=chain_recv_sem.at[slot],
-            device_id=z_device(way),
+            device_id=z_device(2 * way if dist == half else way),
             device_id_type=MESH,
         )
 
     def chain_step(kind, way, dist):
         index = order.index(half if dist == half else way * dist)
         value = (part_k if kind == "k" else part_v)[index]
-        if dist < lines[(kind, way)]:
-            chain_copy(kind, way, dist + 1).wait_recv()
-            value = value + chain_recv[slots[(kind, way, dist + 1)]].astype(F32)
+        joined = [dist + 1] if dist < half - 1 else []
+        if dist == half - 2 and (kind, way, half) in slots:
+            joined.append(half)
+        for earlier in joined:
+            chain_copy(kind, way, earlier).wait_recv()
+            value = value + chain_recv[slots[(kind, way, earlier)]].astype(F32)
         chain_send[slots[(kind, way, dist)]] = value.astype(BF16)
         chain_copy(kind, way, dist).start()
 
     events = {at: [] for at in range(size_z + 1)}
-    for (kind, way), first_dist in lines.items():
-        for dist in range(first_dist, 0, -1):
-            at = order.index(half if dist == half else way * dist)
-            if first_dist == half and dist < half:
-                at = 4 + 3 * (half - 1 - dist)
-            elif dist < half - 1:
-                at = 5 + 3 * (half - 2 - dist) + (way < 0)
-            events[min(at, size_z) if dist > 1 else size_z].append((kind, way, dist))
-    for listed in events.values():
-        listed.sort(key=lambda e: lines[(e[0], e[1])] - half)
+    events[1] = [("k", 1, 4), ("v", -1, 4)]
+    events[2] = [("k", 1, 3)]
+    events[3] = [("v", -1, 3), ("v", 1, 3), ("k", -1, 3)]
+    events[6] = [("k", 1, 2), ("v", -1, 2)]
+    events[7] = [("v", 1, 2), ("k", -1, 2)]
+    events[8] = [("k", 1, 1), ("v", -1, 1), ("v", 1, 1), ("k", -1, 1)]
 
     def dist_at(index):
         near = half - index // 2
@@ -511,7 +519,6 @@
             pltpu.VMEM((size_z, key_count, HEAD_DIM), BF16),
             pltpu.VMEM((own, columns), BF16),
             pltpu.VMEM((own, columns), BF16),
-            pltpu.VMEM((own, columns), BF16),
             pltpu.VMEM((own, heads_all), F32),
             pltpu.VMEM((own, 128), F32),
             pltpu.VMEM((2 * heads_all, rows), F32),
@@ -525,8 +532,9 @@
             pltpu.VMEM((size_z, key_count, HEAD_DIM), F32),
             pltpu.VMEM((chain, key_count, HEAD_DIM), BF16),
             pltpu.VMEM((chain, key_count, HEAD_DIM), BF16),
-            dma((9,)),
+            dma((8,)),
             dma((3,)),
+            pltpu.SemaphoreType.REGULAR,
             pltpu.SemaphoreType.REGULAR,
             dma,
             dma,

time: 43.4 us -> 42.5 us (0.979); the launches traced: 42.6 us -> 42.2 us
  Pallas kernels: 42 us -> 41.5 us
    pallas_call x1, Pallas kernels: 40 us -> 39.6 us  [local(): pl.pallas_call(functools.partial(kernel, sizes), out_shape=(jax.ShapeDtyp...]
where the time goes in v4:
time: 42.5 us; the launch traced here: 42.2 us
  Pallas kernels  41.5 us (98%)
  between operations  0.64 us (2%)
    pallas_call x1, Pallas kernels, local(): pl.pallas_call(functools.partial(kernel, sizes), out_shape=(jax.ShapeDtyp...  39.6 us
    pallas_call x1, Pallas kernels, add_up(): pl.pallas_call(add_up_kernel, out_shape=(jax.ShapeDtypeStruct(dq_recv.sha...  1.94 us

profile of v4, /device:TPU:32, one launch (start us, length us, event | category | flops | bytes accessed | tf_op | source)
XLA Modules:
  0.0 42.2 jit_solution(18422764348781246139)
XLA Ops:
  0.6 39.6 %shard_map.112 = (bf16[4,16,3072]{2,1,0:T(8,128)(2,1)}, f32[256,128]{1,0:T(8,128)}, f32[256,128]{1,0:T(8,128)}, bf16[2,256,128]{2,1,0:T(8,128)(2,1)}, bf16[2,256,128]{2,1,0:T(8,128)(2,1)}) custom-call(bf16[16,3072]{1,0:T(8,128)(2,1)} %q_hbm.1, bf16[256,128]{1,0:T(8,128)(2,1)} %k_hbm.1, bf16[256,128]{1,0:T(8,128)(2,1)} %v_hbm.1, bf16[16,3072]{1,0:T(8,128)(2,1)} %o_hbm.1, ...), custom_call_target="tpu_custom_call" | custom-call | tf_op jit(solution)/shard_map/pallas_call | solution.py:504
  40.2 1.9 %add_up.1 = (bf16[16,3072]{1,0:T(8,128)(2,1)}, bf16[256,128]{1,0:T(8,128)(2,1)}, bf16[256,128]{1,0:T(8,128)(2,1)}) custom-call(bf16[4,16,3072]{2,1,0:T(8,128)(2,1)} %get-tuple-element.8.dq_recv, f32[256,128]{1,0:T(8,128)} %get-tuple-element.9.own_k, f32[256,128]{1,0:T(8,128)} %get-tuple-element.10.own_v, bf16[2,256,128]{2,1,0:T(8,128)(2,1)} %get-tuple-element.11.recv_k, ...), custom_call_target="tpu_custom_call" | custom-call | tf_op jit(solution)/shard_map/add_up/pallas_call | solution.py:468

commit v5 on v4

--- a/solution.py
+++ b/solution.py
@@ -375,11 +375,11 @@
 
     events = {at: [] for at in range(size_z + 1)}
     events[1] = [("k", 1, 4), ("v", -1, 4)]
-    events[2] = [("k", 1, 3)]
-    events[3] = [("v", -1, 3), ("v", 1, 3), ("k", -1, 3)]
-    events[6] = [("k", 1, 2), ("v", -1, 2)]
-    events[7] = [("v", 1, 2), ("k", -1, 2)]
-    events[8] = [("k", 1, 1), ("v", -1, 1), ("v", 1, 1), ("k", -1, 1)]
+    events[2] = [("v", 1, 3)]
+    events[3] = [("k", -1, 3), ("k", 1, 3), ("v", -1, 3)]
+    events[6] = [("v", 1, 2), ("k", -1, 2)]
+    events[7] = [("k", 1, 2), ("v", -1, 2)]
+    events[8] = [("v", 1, 1), ("k", -1, 1), ("k", 1, 1), ("v", -1, 1)]
 
     def dist_at(index):
         near = half - index // 2
@@ -475,8 +475,8 @@
         in_specs=[vmem] * 5,
         out_specs=(vmem,) * 3,
         name="add_up",
-        compiler_params=pltpu.CompilerParams(vmem_limit_bytes=60 * 1024 * 1024),
-    )(*terms)
+        compiler_params=pltpu.CompilerParams(vmem_limit_bytes=32 * 1024 * 1024),
+    )(*(pltpu.with_memory_space_constraint(term, pltpu.VMEM) for term in terms))
 
 
 def local(
@@ -504,14 +504,14 @@
     terms = pl.pallas_call(
         functools.partial(kernel, sizes),
         out_shape=(
-            jax.ShapeDtypeStruct((size_x,) + query_rows.shape, BF16),
-            jax.ShapeDtypeStruct(key_rows.shape, F32),
-            jax.ShapeDtypeStruct(value_rows.shape, F32),
-            jax.ShapeDtypeStruct((2,) + key_rows.shape, BF16),
-            jax.ShapeDtypeStruct((2,) + value_rows.shape, BF16),
+            pltpu.VMEM((size_x,) + query_rows.shape, BF16),
+            pltpu.VMEM(key_rows.shape, F32),
+            pltpu.VMEM(value_rows.shape, F32),
+            pltpu.VMEM((2,) + key_rows.shape, BF16),
+            pltpu.VMEM((2,) + value_rows.shape, BF16),
         ),
         in_specs=[hbm] * 9,
-        out_specs=(hbm,) * 5,
+        out_specs=(pl.BlockSpec(memory_space=pltpu.VMEM),) * 5,
         scratch_shapes=[
             pltpu.VMEM((rows, 2 * width), BF16),
             pltpu.VMEM((rows, 128), F32),
@@ -549,18 +549,23 @@
             dma((2,)),
         ],
         compiler_params=pltpu.CompilerParams(
-            collective_id=0, has_side_effects=True, vmem_limit_bytes=60 * 1024 * 1024
+            collective_id=0, has_side_effects=True, vmem_limit_bytes=32 * 1024 * 1024
         ),
     )(
-        query_rows,
-        key_rows,
-        value_rows,
-        output_rows,
-        grad_out,
-        log_norm,
-        mask_table.T,
-        key_order,
-        query_order,
+        *(
+            pltpu.with_memory_space_constraint(operand, pltpu.HBM)
+            for operand in (
+                query_rows,
+                key_rows,
+                value_rows,
+                output_rows,
+                grad_out,
+                log_norm,
+                mask_table.T,
+                key_order,
+                query_order,
+            )
+        )
     )
     return add_up(terms)
 

time: 42.5 us -> 41.4 us (0.974)
  Pallas kernels: 41.5 us -> 40.6 us
    pallas_call x1, Pallas kernels: 1.94 us -> 0.75 us  [add_up(): pl.pallas_call(add_up_kernel, out_shape=(jax.ShapeDtypeStruct(dq_recv.sha...]
where the time goes in v5:
time: 41.4 us; the launch traced here: 41.3 us
  Pallas kernels  40.6 us (98%)
  between operations  0.64 us (2%)
    pallas_call x1, Pallas kernels, local(): pl.pallas_call(functools.partial(kernel, sizes), out_shape=(pltpu.VMEM((s...  39.9 us

profile of v5, /device:TPU:32, one launch (start us, length us, event | category | flops | bytes accessed | tf_op | source)
XLA Modules:
  0.0 41.3 jit_solution(5850543560420545981)
XLA Ops:
  0.6 39.9 %shard_map.112 = (bf16[4,16,3072]{2,1,0:T(8,128)(2,1)S(1)}, f32[256,128]{1,0:T(8,128)S(1)}, f32[256,128]{1,0:T(8,128)S(1)}, bf16[2,256,128]{2,1,0:T(8,128)(2,1)S(1)}, bf16[2,256,128]{2,1,0:T(8,128)(2,1)S(1)}) custom-call(bf16[16,3072]{1,0:T(8,128)(2,1)} %q_hbm.1, bf16[256,128]{1,0:T(8,128)(2,1)} %k_hbm.1, bf16[256,128]{1,0:T(8,128)(2,1)} %v_hbm.1, ...), custom_call_target="tpu_custom_call" | custom-call | tf_op jit(solution)/shard_map/pallas_call | solution.py:504
  40.5 0.7 %add_up.1 = (bf16[16,3072]{1,0:T(8,128)(2,1)}, bf16[256,128]{1,0:T(8,128)(2,1)}, bf16[256,128]{1,0:T(8,128)(2,1)}) custom-call(bf16[4,16,3072]{2,1,0:T(8,128)(2,1)S(1)} %get-tuple-element.8.dq_recv, f32[256,128]{1,0:T(8,128)S(1)} %get-tuple-element.9.own_k, f32[256,128]{1,0:T(8,128)S(1)} %get-tuple-element.10.own_v, ...), custom_call_target="tpu_custom_call" | custom-call | tf_op jit(solution)/shard_map/add_up/pallas_call | solution.py:468

commit v6 on v5

--- a/solution.py
+++ b/solution.py
@@ -234,6 +234,12 @@
     for copy in own_copies:
         copy.start()
 
+    pl.semaphore_wait(relay_sem, 2)
+    for way in (1, -1):
+        pl.semaphore_signal(
+            relay_x_sem, inc=1, device_id=device(0, way, 0), device_id_type=MESH
+        )
+    send_rows(0, 2)
     for copy in loads:
         copy.wait()
 
@@ -252,19 +258,12 @@
         send_nd(*peer)
     own_copies.append(pltpu.make_async_copy(nd_own, nd_all.at[my_rows], own_sem.at[0]))
     own_copies[-1].start()
-    pl.semaphore_wait(relay_sem, 2)
-    for way in (1, -1):
-        pl.semaphore_signal(
-            relay_x_sem, inc=1, device_id=device(0, way, 0), device_id_type=MESH
-        )
-    send_rows(0, 2)
     send_nd(0, 2)
 
     pl.semaphore_wait(relay_x_sem, 2)
-    for tx in (1, -1):
-        for ty in (1, -1, 2):
-            send_rows(tx, ty)
-            send_nd(tx, ty)
+    for tx, ty in ((1, -1), (-1, 1), (-1, 2), (1, 1), (-1, -1), (1, 2)):
+        send_rows(tx, ty)
+        send_nd(tx, ty)
     ring_step(2)
     if half > 2:
         ring_step(3)
@@ -403,7 +402,7 @@
 
         return carry
 
-    lax.fori_loop(0, size_z, block_step, 0)
+    lax.fori_loop(0, size_z, block_step, 0, unroll=2)
 
     stores = [
         pltpu.make_async_copy(part_k.at[0], own_k, store_sem.at[0]),

time: 41.4 us -> 41.2 us (level)
  no operation moved by 1% of the time
where the time goes in v6:
time: 41.2 us; the launch traced here: 41.1 us
  Pallas kernels  40.4 us (98%)
  between operations  0.64 us (2%)
    pallas_call x1, Pallas kernels, local(): pl.pallas_call(functools.partial(kernel, sizes), out_shape=(pltpu.VMEM((s...  39.7 us

profile of v6, /device:TPU:32, one launch (start us, length us, event | category | flops | bytes accessed | tf_op | source)
XLA Modules:
  0.0 41.1 jit_solution(768029205178545271)
XLA Ops:
  0.6 39.7 %shard_map.112 = (bf16[4,16,3072]{2,1,0:T(8,128)(2,1)S(1)}, f32[256,128]{1,0:T(8,128)S(1)}, f32[256,128]{1,0:T(8,128)S(1)}, bf16[2,256,128]{2,1,0:T(8,128)(2,1)S(1)}, bf16[2,256,128]{2,1,0:T(8,128)(2,1)S(1)}) custom-call(bf16[16,3072]{1,0:T(8,128)(2,1)} %q_hbm.1, bf16[256,128]{1,0:T(8,128)(2,1)} %k_hbm.1, bf16[256,128]{1,0:T(8,128)(2,1)} %v_hbm.1, ...), custom_call_target="tpu_custom_call" | custom-call | tf_op jit(solution)/shard_map/pallas_call | solution.py:503
  40.3 0.7 %add_up.1 = (bf16[16,3072]{1,0:T(8,128)(2,1)}, bf16[256,128]{1,0:T(8,128)(2,1)}, bf16[256,128]{1,0:T(8,128)(2,1)}) custom-call(bf16[4,16,3072]{2,1,0:T(8,128)(2,1)S(1)} %get-tuple-element.8.dq_recv, f32[256,128]{1,0:T(8,128)S(1)} %get-tuple-element.9.own_k, f32[256,128]{1,0:T(8,128)S(1)} %get-tuple-element.10.own_v, ...), custom_call_target="tpu_custom_call" | custom-call | tf_op jit(solution)/shard_map/add_up/pallas_call | solution.py:467

commit v7 on v6

--- a/solution.py
+++ b/solution.py
@@ -50,6 +50,7 @@
     g_own,
     norm_own,
     nd_own,
+    nd_send,
     nd_rows,
     table,
     key_order,
@@ -200,7 +201,10 @@
             )
 
     def send_nd(tx, ty):
-        plane_copy(nd_own, nd_all.at[my_rows], nd_send_sem, nd_recv_sem, tx, ty, 0, 0)
+        group = (my_y + ty + size_y) % size_y
+        plane_copy(
+            nd_send.at[group], nd_all.at[my_rows], nd_send_sem, nd_recv_sem, tx, ty, 0, 0
+        )
 
     def wait_chunk(sx, sy):
         at = chunk_rows(sx, sy)
@@ -240,6 +244,10 @@
             relay_x_sem, inc=1, device_id=device(0, way, 0), device_id_type=MESH
         )
     send_rows(0, 2)
+    pl.semaphore_wait(relay_x_sem, 2)
+    passed_on = ((1, -1), (-1, 1), (-1, 2), (1, 1), (-1, -1), (1, 2))
+    for peer in passed_on:
+        send_rows(*peer)
     for copy in loads:
         copy.wait()
 
@@ -252,18 +260,30 @@
         )
         tile = jnp.where(lane == heads_all + head, delta, tile)
     nd_own[...] = tile
-    nd_own[:, 0:heads_all] = norm_own[...] * log2e
+    nd_own[:, 0:heads_all] = jnp.clip(norm_own[...] * log2e, -1e30, 1e30)
+    both = nd_own[...]
+    for group in range(size_y):
+        first = group * heads_loc
+        norms = pltpu.roll(both, (128 - first) % 128, 1)
+        deltas = pltpu.roll(both, (128 - heads_all - first + heads_loc) % 128, 1)
+        value = jnp.where(
+            lane < heads_loc, norms, jnp.where(lane < 2 * heads_loc, deltas, 0.0)
+        )
+        packed = jnp.zeros_like(value)
+        for term in range(3):
+            rounded = value.astype(BF16).astype(F32)
+            value = value - rounded
+            packed = packed + (pltpu.roll(rounded, 16 * term, 1) if term else rounded)
+        nd_send[group] = packed.astype(BF16)
 
     for peer in beside:
         send_nd(*peer)
-    own_copies.append(pltpu.make_async_copy(nd_own, nd_all.at[my_rows], own_sem.at[0]))
+    own_copies.append(pltpu.make_async_copy(nd_send.at[my_y], nd_all.at[my_rows], own_sem.at[0]))
     own_copies[-1].start()
+    for peer in passed_on:
+        send_nd(*peer)
     send_nd(0, 2)
 
-    pl.semaphore_wait(relay_x_sem, 2)
-    for tx, ty in ((1, -1), (-1, 1), (-1, 2), (1, 1), (-1, -1), (1, 2)):
-        send_rows(tx, ty)
-        send_nd(tx, ty)
     ring_step(2)
     if half > 2:
         ring_step(3)
@@ -301,8 +321,8 @@
         wait_chunk(2, sy)
     for copy in own_copies:
         copy.wait()
-    turned = nd_all[...].T
-    nd_rows[...] = turned[0 : 2 * heads_all]
+    turned = nd_all[...].astype(F32).T
+    nd_rows[...] = turned[0:16] + turned[16:32] + turned[32:48]
 
     order = [0, half]
     for distance in range(half - 1, 0, -1):
@@ -327,8 +347,8 @@
         dscores = []
         for head in range(heads_loc):
             cols = pl.ds(head * HEAD_DIM, HEAD_DIM)
-            norm = nd_rows[pl.ds(my_y * heads_loc + head, 1), :]
-            delta = nd_rows[pl.ds(heads_all + my_y * heads_loc + head, 1), :]
+            norm = nd_rows[pl.ds(head, 1), :]
+            delta = nd_rows[pl.ds(heads_loc + head, 1), :]
             scores = dot_nt(key_blk, qg_all[:, cols])
             weights = jnp.exp2(jnp.minimum(scores * (score_scale * log2e) - norm, bias[...]))
             dprobs = dot_nt(value_blk, qg_all[:, pl.ds(width + head * HEAD_DIM, HEAD_DIM)])
@@ -513,14 +533,15 @@
         out_specs=(pl.BlockSpec(memory_space=pltpu.VMEM),) * 5,
         scratch_shapes=[
             pltpu.VMEM((rows, 2 * width), BF16),
-            pltpu.VMEM((rows, 128), F32),
+            pltpu.VMEM((rows, 128), BF16),
             pltpu.VMEM((size_z, key_count, HEAD_DIM), BF16),
             pltpu.VMEM((size_z, key_count, HEAD_DIM), BF16),
             pltpu.VMEM((own, columns), BF16),
             pltpu.VMEM((own, columns), BF16),
             pltpu.VMEM((own, heads_all), F32),
             pltpu.VMEM((own, 128), F32),
-            pltpu.VMEM((2 * heads_all, rows), F32),
+            pltpu.VMEM((size_y, own, 128), BF16),
+            pltpu.VMEM((16, rows), F32),
             pltpu.SMEM(mask_table.shape[::-1], jnp.int32),
             pltpu.SMEM(key_order.shape, jnp.int32),
             pltpu.SMEM(query_order.shape, jnp.int32),

time: 41.2 us -> 41.1 us (level)
  no operation moved by 1% of the time
where the time goes in v7:
time: 41.1 us; the launch traced here: 41 us
  Pallas kernels  40.3 us (98%)
  between operations  0.64 us (2%)
    pallas_call x1, Pallas kernels, local(): pl.pallas_call(functools.partial(kernel, sizes), out_shape=(pltpu.VMEM((s...  39.6 us

profile of v7, /device:TPU:32, one launch (start us, length us, event | category | flops | bytes accessed | tf_op | source)
XLA Modules:
  0.0 41.0 jit_solution(9647016906397824808)
XLA Ops:
  0.6 39.6 %shard_map.112 = (bf16[4,16,3072]{2,1,0:T(8,128)(2,1)S(1)}, f32[256,128]{1,0:T(8,128)S(1)}, f32[256,128]{1,0:T(8,128)S(1)}, bf16[2,256,128]{2,1,0:T(8,128)(2,1)S(1)}, bf16[2,256,128]{2,1,0:T(8,128)(2,1)S(1)}) custom-call(bf16[16,3072]{1,0:T(8,128)(2,1)} %q_hbm.1, bf16[256,128]{1,0:T(8,128)(2,1)} %k_hbm.1, bf16[256,128]{1,0:T(8,128)(2,1)} %v_hbm.1, ...), custom_call_target="tpu_custom_call" | custom-call | tf_op jit(solution)/shard_map/pallas_call | solution.py:523
  40.2 0.7 %add_up.1 = (bf16[16,3072]{1,0:T(8,128)(2,1)}, bf16[256,128]{1,0:T(8,128)(2,1)}, bf16[256,128]{1,0:T(8,128)(2,1)}) custom-call(bf16[4,16,3072]{2,1,0:T(8,128)(2,1)S(1)} %get-tuple-element.8.dq_recv, f32[256,128]{1,0:T(8,128)S(1)} %get-tuple-element.9.own_k, f32[256,128]{1,0:T(8,128)S(1)} %get-tuple-element.10.own_v, ...), custom_call_target="tpu_custom_call" | custom-call | tf_op jit(solution)/shard_map/add_up/pallas_call | solution.py:487
